TPU v7x, 256 devices: a whole 4x4x8 slice. The times are simulated.
256 devices in a mesh: ctx: 32 (over z, y), head: 8 (over x, core).
Axes of the slice: x: 4, y: 4, z: 8, core: 2. Of those that a mesh axis runs over, the one named last changes fastest.
Arguments:
- queries: bfloat16 [16384, 2048], P('ctx', 'head'), may hold values from -6 to 6
- key_vec: bfloat16 [16384, 2048], P('ctx', 'head'), may hold values from -6 to 6
- values: bfloat16 [16384, 4096], P('ctx', 'head'), may hold values from -6 to 6
- out_gate: bfloat16 [16384, 4096], P('ctx', 'head'), may hold values from -6 to 6
- beta_logit: float32 [32, 16384], P('head', 'ctx'), may hold values from -6 to 6
- decay_gate: float32 [32, 16384], P('head', 'ctx'), may hold values from 0 to 196608, as said below
- decay_exp: int32 [32], P('head'), may hold values from -4 to 9, as said below
- norm_gain: float32 [128], replicated, may hold values from 0.25 to 1.75
- out_weight: bfloat16 [4096, 2048], P('head'), may hold values from -0.09375 to 0.09375
- router_weight: bfloat16 [2048, 512], replicated, may hold values from -0.75 to 0.75
- old_scores: int32 [16384, 512], P(('ctx', 'head')), may hold values from -8192 to 8192
Outputs:
- layer_out: bfloat16 [16384, 2048], P(('ctx', 'head'))
- divergence: float32 [16384], P(('ctx', 'head'))
Inputs may be any that keep to these rules, and one draw needn't show every extreme that they name: `decay_exp`: every whole number from min to max is the exponent of some head. `decay_gate`: positive.
All inputs are finite; a program needn't handle non-finite values.
Results may differ from a plain program's by a relative error of at most 0.005.
Values may be sent and summed in bfloat16 or wider, within the bound.
A program may use at most 128 MiB of HBM per device.

v0:
```python
import jax
import jax.numpy as jnp
from jax import lax
from jax.sharding import PartitionSpec as P

KEY_DIM = 128
VALUE_DIM = 128
BLOCK_LEN = 64


epsilon = 1e-06
highest = lax.Precision.HIGHEST


def from_behind(x, axis, by):
    length = lax.axis_size(axis)
    pairs = [(i, i + by) for i in range(length) if 0 <= i + by < length]
    return lax.ppermute(x, axis, pairs)


def product_matrix(pattern, first_op, second_op):
    return jnp.einsum(pattern, first_op, second_op, precision=highest)


def prepare(queries, key_vec, values, beta_logit, decay_gate, decay_exp, chain_length):
    token_count = queries.shape[0]
    query_heads = queries.astype(jnp.float32).reshape(token_count, -1, KEY_DIM)
    key_heads = key_vec.astype(jnp.float32).reshape(token_count, -1, KEY_DIM)
    unit_query = (
        query_heads
        / jnp.sqrt(jnp.sum(query_heads * query_heads, -1, keepdims=True) + epsilon)
        / KEY_DIM**0.5
    )
    unit_key = key_heads / jnp.sqrt(jnp.sum(key_heads * key_heads, -1, keepdims=True) + epsilon)
    unit_query = jnp.repeat(unit_query, 2, axis=1)
    unit_key = jnp.repeat(unit_key, 2, axis=1)
    head_count = unit_query.shape[1]
    blocks = token_count // BLOCK_LEN
    value_heads = values.astype(jnp.float32).reshape(token_count, head_count, VALUE_DIM)

    def arrange(tensor):
        return tensor.reshape(blocks, BLOCK_LEN, head_count, -1).transpose(2, 0, 1, 3)

    beta = jax.nn.sigmoid(beta_logit).reshape(head_count, blocks, BLOCK_LEN)
    rate = jnp.exp2(decay_exp.astype(jnp.float32)) / chain_length
    log_decay = (-rate[:, None] * decay_gate).reshape(head_count, blocks, BLOCK_LEN)
    return (arrange(unit_query), arrange(unit_key), arrange(value_heads), beta, log_decay)


def block_pass(query_blocks, key_blocks, value_blocks, beta, log_decay):
    head_count = query_blocks.shape[0]
    block_len = query_blocks.shape[2]
    value_width = value_blocks.shape[-1]
    key_width = key_blocks.shape[-1]
    position = jnp.arange(block_len)
    strict = position[:, None] > position[None, :]
    inclusive = position[:, None] >= position[None, :]
    cumulative = jnp.cumsum(log_decay, axis=-1)
    growth_factor = jnp.exp(cumulative)
    fade = jnp.exp(jnp.minimum(cumulative[..., :, None] - cumulative[..., None, :], 0.0))
    key_gram = product_matrix("hnid,hnjd->hnij", key_blocks, key_blocks)
    system = jnp.eye(block_len, dtype=jnp.float32) + beta[..., None] * jnp.where(
        strict, key_gram * fade, 0.0
    )
    right_side = jnp.concatenate(
        [beta[..., None] * value_blocks, (beta * growth_factor)[..., None] * key_blocks], axis=-1
    )
    solved = jax.scipy.linalg.solve_triangular(system, right_side, lower=True, unit_diagonal=True)
    written_values = solved[..., :value_width]
    widened_keys = solved[..., value_width:]
    score_matrix = jnp.where(
        inclusive, product_matrix("hnid,hnjd->hnij", query_blocks, key_blocks) * fade, 0.0
    )
    key_remainder = jnp.exp(cumulative[..., -1:] - cumulative)[..., None] * key_blocks
    final_growth = growth_factor[..., -1]
    leading = growth_factor[..., None] * query_blocks - product_matrix(
        "hnij,hnjk->hnik", score_matrix, widened_keys
    )

    def advance(carry, inputs):
        memory_state, propagator = carry
        (
            current_query,
            current_growth,
            current_written,
            current_widened,
            scores_now,
            current_remainder,
            current_final,
            leading_now,
        ) = inputs
        current_final = current_final[:, None, None]
        fresh_values = current_written - product_matrix(
            "pjz,pzw->pjw", current_widened, memory_state
        )
        current_output = current_growth[..., None] * product_matrix(
            "pjz,pzw->pjw", current_query, memory_state
        ) + product_matrix("gxd,gdk->gxk", scores_now, fresh_values)
        updated_memory = current_final * memory_state + product_matrix(
            "pgy,pgq->pyq", current_remainder, fresh_values
        )
        carried_state = product_matrix("hck,hkm->hcm", leading_now, propagator)
        new_propagator = current_final * propagator - product_matrix(
            "hck,hcm->hkm",
            current_remainder,
            product_matrix("hck,hkm->hcm", current_widened, propagator),
        )
        return ((updated_memory, new_propagator), (current_output, carried_state))

    start_memory = jnp.zeros((head_count, key_width, value_width), jnp.float32)
    start_map = jnp.broadcast_to(
        jnp.eye(key_width, dtype=jnp.float32), (head_count, key_width, key_width)
    )
    sequence = tuple(
        (
            jnp.moveaxis(tensor, 1, 0)
            for tensor in (
                query_blocks,
                growth_factor,
                written_values,
                widened_keys,
                score_matrix,
                key_remainder,
                final_growth,
                leading,
            )
        )
    )
    return lax.scan(advance, (start_memory, start_map), sequence)


def finish(attended, out_gate, norm_gain):
    token_count, head_count = (attended.shape[0], attended.shape[1])
    gate_heads = out_gate.astype(jnp.float32).reshape(token_count, head_count, VALUE_DIM)
    scale = lax.rsqrt(jnp.mean(attended * attended, -1, keepdims=True) + epsilon)
    normed = attended * scale * norm_gain * jax.nn.silu(gate_heads)
    return normed.astype(jnp.bfloat16).reshape(token_count, head_count * VALUE_DIM)


def router_divergence(layer_out, router_weight, old_scores):
    new_logit = jnp.dot(layer_out, router_weight, preferred_element_type=jnp.float32)
    new_logp = new_logit - jnp.log(jnp.sum(jnp.exp(new_logit), -1, keepdims=True))
    old_logit = old_scores.astype(jnp.float32) / 1024.0
    old_logp = old_logit - jnp.log(jnp.sum(jnp.exp(old_logit), -1, keepdims=True))
    return jnp.sum(jnp.exp(old_logp) * (old_logp - new_logp), -1)


def local(
    queries,
    key_vec,
    values,
    out_gate,
    beta_logit,
    decay_gate,
    decay_exp,
    norm_gain,
    out_weight,
    router_weight,
    old_scores,
):
    ctx_count = lax.axis_size("ctx")
    token_count = queries.shape[0]
    prepared = prepare(
        queries, key_vec, values, beta_logit, decay_gate, decay_exp, token_count * ctx_count
    )
    final_carry, stacked = block_pass(*prepared)
    closing_state, closing_map = final_carry
    output_rows, carried_state = stacked

    def relay_step(turn, incoming_state):
        leaving_state = product_matrix("ida,iaj->idj", closing_map, incoming_state) + closing_state
        return from_behind(leaving_state, "ctx", 1)

    incoming_state = lax.fori_loop(0, ctx_count - 1, relay_step, jnp.zeros_like(closing_state))
    head_count = output_rows.shape[1]
    local_output = output_rows + product_matrix("eldg,lgp->eldp", carried_state, incoming_state)
    attended = local_output.transpose(0, 2, 1, 3).reshape(token_count, head_count, VALUE_DIM)
    normed = finish(attended, out_gate, norm_gain)
    summed = lax.psum_scatter(
        jnp.dot(normed, out_weight, preferred_element_type=jnp.float32),
        "head",
        scatter_dimension=0,
        tiled=True,
    )
    layer_out = summed.astype(jnp.bfloat16)
    return (layer_out, router_divergence(layer_out, router_weight, old_scores))


def solution(mesh):
    placed = (
        P("ctx", "head"),
        P("ctx", "head"),
        P("ctx", "head"),
        P("ctx", "head"),
        P("head", "ctx"),
        P("head", "ctx"),
        P("head"),
        P(),
        P("head", None),
        P(),
        P(("ctx", "head"), None),
    )
    return jax.shard_map(
        local,
        mesh=mesh,
        in_specs=placed,
        out_specs=(P(("ctx", "head"), None), P(("ctx", "head"))),
        check_vma=False,
    )
```

profile of v0, /device:TPU:192, one launch (start us, length us, event | category | flops | bytes accessed | tf_op | source)
XLA Modules:
  0.0 734.8 jit_solution(11807180429585699782)
XLA Ops:
  22.5 158.7 %custom-call.4 = f32[4,8,1,64,64]{3,4,2,1,0:T(8,128)} custom-call(f32[4,8,1,64,64]{4,3,2,1,0:T(8,128)} %fusion.46), custom_call_target="InvertDiagBlocksLowerTriangular" | custom-call | tf_op jit(solution)/shard_map/jit(_solve_triangular)/vmap(vmap())/triangular_solve | solution.py:68
  200.0 86.0 %while.28 = (s32[]{:T(128)}, f32[4,128,128]{2,1,0:T(8,128)S(1)}, f32[4,128,128]{2,1,0:T(8,128)S(1)}, f32[8,4,64,128]{3,2,0,1:T(8,128)}, f32[8,4,64,128]{3,2,0,1:...) while((s32[]{:T(128)}, f32[4,128,128]{2,1,0:T(8,128)S(1)}, ...), condition=%wide.region_4.5_spmd.clone, body=%wide.region_3.4_spmd.clone.sunk | while | flops 327712768 | bytes 4333793 | solution.py:129
  286.0 357.0 %while.27 = (s32[]{:T(128)}, f32[4,128,128]{2,1,0:T(8,128)S(1)}, f32[4,128,128]{2,1,0:T(8,128)S(1)}, f32[4,128,128]{2,1,0:T(8,128)S(1)}, s32[]{:T(128)}) while((s32[]{:T(128)}, f32[4,128,128]{2,1,0:T(8,128)S(1)}, f32[4,128,128]{2,1,0:T(8,128)S(1)}, f32[4,128,128]{2,1,0:T(8,128)S(1)}, s32[]{:T(128)}) %tuple.54), condition=%wide.region_6.7_spmd, body=%wide.region_5.6_spmd.sunk | while | flops 100728832 | bytes 2097253 | solution.py:174
  289.9 8.6 %collective-permute-done = f32[4,128,128]{2,1,0:T(8,128)S(1)} collective-permute-done((f32[4,128,128]{2,1,0:T(8,128)S(1)}, f32[4,128,128]{2,1,0:T(8,128)S(1)}, u32[]{:S(2)}, u32[]{:S(2)}) %collective-permute-start) | collective-permute-done | bytes 262176 | tf_op jit(solution)/shard_map/while/body/eval_jaxpr/ppermute | solution.py:18
  300.8 9.2 %collective-permute-done = f32[4,128,128]{2,1,0:T(8,128)S(1)} collective-permute-done((f32[4,128,128]{2,1,0:T(8,128)S(1)}, f32[4,128,128]{2,1,0:T(8,128)S(1)}, u32[]{:S(2)}, u32[]{:S(2)}) %collective-permute-start) | collective-permute-done | bytes 262176 | tf_op jit(solution)/shard_map/while/body/eval_jaxpr/ppermute | solution.py:18
  312.4 8.4 %collective-permute-done = f32[4,128,128]{2,1,0:T(8,128)S(1)} collective-permute-done((f32[4,128,128]{2,1,0:T(8,128)S(1)}, f32[4,128,128]{2,1,0:T(8,128)S(1)}, u32[]{:S(2)}, u32[]{:S(2)}) %collective-permute-start) | collective-permute-done | bytes 262176 | tf_op jit(solution)/shard_map/while/body/eval_jaxpr/ppermute | solution.py:18
  323.1 8.4 %collective-permute-done = f32[4,128,128]{2,1,0:T(8,128)S(1)} collective-permute-done((f32[4,128,128]{2,1,0:T(8,128)S(1)}, f32[4,128,128]{2,1,0:T(8,128)S(1)}, u32[]{:S(2)}, u32[]{:S(2)}) %collective-permute-start) | collective-permute-done | bytes 262176 | tf_op jit(solution)/shard_map/while/body/eval_jaxpr/ppermute | solution.py:18
  333.9 8.4 %collective-permute-done = f32[4,128,128]{2,1,0:T(8,128)S(1)} collective-permute-done((f32[4,128,128]{2,1,0:T(8,128)S(1)}, f32[4,128,128]{2,1,0:T(8,128)S(1)}, u32[]{:S(2)}, u32[]{:S(2)}) %collective-permute-start) | collective-permute-done | bytes 262176 | tf_op jit(solution)/shard_map/while/body/eval_jaxpr/ppermute | solution.py:18
  344.7 8.4 %collective-permute-done = f32[4,128,128]{2,1,0:T(8,128)S(1)} collective-permute-done((f32[4,128,128]{2,1,0:T(8,128)S(1)}, f32[4,128,128]{2,1,0:T(8,128)S(1)}, u32[]{:S(2)}, u32[]{:S(2)}) %collective-permute-start) | collective-permute-done | bytes 262176 | tf_op jit(solution)/shard_map/while/body/eval_jaxpr/ppermute | solution.py:18
  355.5 9.1 %collective-permute-done = f32[4,128,128]{2,1,0:T(8,128)S(1)} collective-permute-done((f32[4,128,128]{2,1,0:T(8,128)S(1)}, f32[4,128,128]{2,1,0:T(8,128)S(1)}, u32[]{:S(2)}, u32[]{:S(2)}) %collective-permute-start) | collective-permute-done | bytes 262176 | tf_op jit(solution)/shard_map/while/body/eval_jaxpr/ppermute | solution.py:18
  366.9 10.2 %collective-permute-done = f32[4,128,128]{2,1,0:T(8,128)S(1)} collective-permute-done((f32[4,128,128]{2,1,0:T(8,128)S(1)}, f32[4,128,128]{2,1,0:T(8,128)S(1)}, u32[]{:S(2)}, u32[]{:S(2)}) %collective-permute-start) | collective-permute-done | bytes 262176 | tf_op jit(solution)/shard_map/while/body/eval_jaxpr/ppermute | solution.py:18
  379.5 11.1 %collective-permute-done = f32[4,128,128]{2,1,0:T(8,128)S(1)} collective-permute-done((f32[4,128,128]{2,1,0:T(8,128)S(1)}, f32[4,128,128]{2,1,0:T(8,128)S(1)}, u32[]{:S(2)}, u32[]{:S(2)}) %collective-permute-start) | collective-permute-done | bytes 262176 | tf_op jit(solution)/shard_map/while/body/eval_jaxpr/ppermute | solution.py:18
  392.9 10.3 %collective-permute-done = f32[4,128,128]{2,1,0:T(8,128)S(1)} collective-permute-done((f32[4,128,128]{2,1,0:T(8,128)S(1)}, f32[4,128,128]{2,1,0:T(8,128)S(1)}, u32[]{:S(2)}, u32[]{:S(2)}) %collective-permute-start) | collective-permute-done | bytes 262176 | tf_op jit(solution)/shard_map/while/body/eval_jaxpr/ppermute | solution.py:18
  405.5 9.4 %collective-permute-done = f32[4,128,128]{2,1,0:T(8,128)S(1)} collective-permute-done((f32[4,128,128]{2,1,0:T(8,128)S(1)}, f32[4,128,128]{2,1,0:T(8,128)S(1)}, u32[]{:S(2)}, u32[]{:S(2)}) %collective-permute-start) | collective-permute-done | bytes 262176 | tf_op jit(solution)/shard_map/while/body/eval_jaxpr/ppermute | solution.py:18
  417.2 8.5 %collective-permute-done = f32[4,128,128]{2,1,0:T(8,128)S(1)} collective-permute-done((f32[4,128,128]{2,1,0:T(8,128)S(1)}, f32[4,128,128]{2,1,0:T(8,128)S(1)}, u32[]{:S(2)}, u32[]{:S(2)}) %collective-permute-start) | collective-permute-done | bytes 262176 | tf_op jit(solution)/shard_map/while/body/eval_jaxpr/ppermute | solution.py:18
  428.0 8.4 %collective-permute-done = f32[4,128,128]{2,1,0:T(8,128)S(1)} collective-permute-done((f32[4,128,128]{2,1,0:T(8,128)S(1)}, f32[4,128,128]{2,1,0:T(8,128)S(1)}, u32[]{:S(2)}, u32[]{:S(2)}) %collective-permute-start) | collective-permute-done | bytes 262176 | tf_op jit(solution)/shard_map/while/body/eval_jaxpr/ppermute | solution.py:18
  438.8 8.4 %collective-permute-done = f32[4,128,128]{2,1,0:T(8,128)S(1)} collective-permute-done((f32[4,128,128]{2,1,0:T(8,128)S(1)}, f32[4,128,128]{2,1,0:T(8,128)S(1)}, u32[]{:S(2)}, u32[]{:S(2)}) %collective-permute-start) | collective-permute-done | bytes 262176 | tf_op jit(solution)/shard_map/while/body/eval_jaxpr/ppermute | solution.py:18
  449.6 8.4 %collective-permute-done = f32[4,128,128]{2,1,0:T(8,128)S(1)} collective-permute-done((f32[4,128,128]{2,1,0:T(8,128)S(1)}, f32[4,128,128]{2,1,0:T(8,128)S(1)}, u32[]{:S(2)}, u32[]{:S(2)}) %collective-permute-start) | collective-permute-done | bytes 262176 | tf_op jit(solution)/shard_map/while/body/eval_jaxpr/ppermute | solution.py:18
  460.4 9.0 %collective-permute-done = f32[4,128,128]{2,1,0:T(8,128)S(1)} collective-permute-done((f32[4,128,128]{2,1,0:T(8,128)S(1)}, f32[4,128,128]{2,1,0:T(8,128)S(1)}, u32[]{:S(2)}, u32[]{:S(2)}) %collective-permute-start) | collective-permute-done | bytes 262176 | tf_op jit(solution)/shard_map/while/body/eval_jaxpr/ppermute | solution.py:18
  471.7 10.1 %collective-permute-done = f32[4,128,128]{2,1,0:T(8,128)S(1)} collective-permute-done((f32[4,128,128]{2,1,0:T(8,128)S(1)}, f32[4,128,128]{2,1,0:T(8,128)S(1)}, u32[]{:S(2)}, u32[]{:S(2)}) %collective-permute-start) | collective-permute-done | bytes 262176 | tf_op jit(solution)/shard_map/while/body/eval_jaxpr/ppermute | solution.py:18
  484.1 11.2 %collective-permute-done = f32[4,128,128]{2,1,0:T(8,128)S(1)} collective-permute-done((f32[4,128,128]{2,1,0:T(8,128)S(1)}, f32[4,128,128]{2,1,0:T(8,128)S(1)}, u32[]{:S(2)}, u32[]{:S(2)}) %collective-permute-start) | collective-permute-done | bytes 262176 | tf_op jit(solution)/shard_map/while/body/eval_jaxpr/ppermute | solution.py:18
  497.7 10.4 %collective-permute-done = f32[4,128,128]{2,1,0:T(8,128)S(1)} collective-permute-done((f32[4,128,128]{2,1,0:T(8,128)S(1)}, f32[4,128,128]{2,1,0:T(8,128)S(1)}, u32[]{:S(2)}, u32[]{:S(2)}) %collective-permute-start) | collective-permute-done | bytes 262176 | tf_op jit(solution)/shard_map/while/body/eval_jaxpr/ppermute | solution.py:18
  510.4 9.6 %collective-permute-done = f32[4,128,128]{2,1,0:T(8,128)S(1)} collective-permute-done((f32[4,128,128]{2,1,0:T(8,128)S(1)}, f32[4,128,128]{2,1,0:T(8,128)S(1)}, u32[]{:S(2)}, u32[]{:S(2)}) %collective-permute-start) | collective-permute-done | bytes 262176 | tf_op jit(solution)/shard_map/while/body/eval_jaxpr/ppermute | solution.py:18
  522.3 8.6 %collective-permute-done = f32[4,128,128]{2,1,0:T(8,128)S(1)} collective-permute-done((f32[4,128,128]{2,1,0:T(8,128)S(1)}, f32[4,128,128]{2,1,0:T(8,128)S(1)}, u32[]{:S(2)}, u32[]{:S(2)}) %collective-permute-start) | collective-permute-done | bytes 262176 | tf_op jit(solution)/shard_map/while/body/eval_jaxpr/ppermute | solution.py:18
  565.6 8.7 %collective-permute-done = f32[4,128,128]{2,1,0:T(8,128)S(1)} collective-permute-done((f32[4,128,128]{2,1,0:T(8,128)S(1)}, f32[4,128,128]{2,1,0:T(8,128)S(1)}, u32[]{:S(2)}, u32[]{:S(2)}) %collective-permute-start) | collective-permute-done | bytes 262176 | tf_op jit(solution)/shard_map/while/body/eval_jaxpr/ppermute | solution.py:18
  576.6 10.2 %collective-permute-done = f32[4,128,128]{2,1,0:T(8,128)S(1)} collective-permute-done((f32[4,128,128]{2,1,0:T(8,128)S(1)}, f32[4,128,128]{2,1,0:T(8,128)S(1)}, u32[]{:S(2)}, u32[]{:S(2)}) %collective-permute-start) | collective-permute-done | bytes 262176 | tf_op jit(solution)/shard_map/while/body/eval_jaxpr/ppermute | solution.py:18
  589.1 9.6 %collective-permute-done = f32[4,128,128]{2,1,0:T(8,128)S(1)} collective-permute-done((f32[4,128,128]{2,1,0:T(8,128)S(1)}, f32[4,128,128]{2,1,0:T(8,128)S(1)}, u32[]{:S(2)}, u32[]{:S(2)}) %collective-permute-start) | collective-permute-done | bytes 262176 | tf_op jit(solution)/shard_map/while/body/eval_jaxpr/ppermute | solution.py:18
  601.0 8.5 %collective-permute-done = f32[4,128,128]{2,1,0:T(8,128)S(1)} collective-permute-done((f32[4,128,128]{2,1,0:T(8,128)S(1)}, f32[4,128,128]{2,1,0:T(8,128)S(1)}, u32[]{:S(2)}, u32[]{:S(2)}) %collective-permute-start) | collective-permute-done | bytes 262176 | tf_op jit(solution)/shard_map/while/body/eval_jaxpr/ppermute | solution.py:18
  611.9 8.4 %collective-permute-done = f32[4,128,128]{2,1,0:T(8,128)S(1)} collective-permute-done((f32[4,128,128]{2,1,0:T(8,128)S(1)}, f32[4,128,128]{2,1,0:T(8,128)S(1)}, u32[]{:S(2)}, u32[]{:S(2)}) %collective-permute-start) | collective-permute-done | bytes 262176 | tf_op jit(solution)/shard_map/while/body/eval_jaxpr/ppermute | solution.py:18
  622.6 8.7 %collective-permute-done = f32[4,128,128]{2,1,0:T(8,128)S(1)} collective-permute-done((f32[4,128,128]{2,1,0:T(8,128)S(1)}, f32[4,128,128]{2,1,0:T(8,128)S(1)}, u32[]{:S(2)}, u32[]{:S(2)}) %collective-permute-start) | collective-permute-done | bytes 262176 | tf_op jit(solution)/shard_map/while/body/eval_jaxpr/ppermute | solution.py:18
  633.7 9.4 %collective-permute-done = f32[4,128,128]{2,1,0:T(8,128)S(1)} collective-permute-done((f32[4,128,128]{2,1,0:T(8,128)S(1)}, f32[4,128,128]{2,1,0:T(8,128)S(1)}, u32[]{:S(2)}, u32[]{:S(2)}) %collective-permute-start) | collective-permute-done | bytes 262176 | tf_op jit(solution)/shard_map/while/body/eval_jaxpr/ppermute | solution.py:18
  653.6 70.2 %reduce-scatter.2.cloned.1.call-done = f32[64,2048]{1,0:T(8,128)} async-done(((f32[512,2048]{1,0:T(8,128)}), f32[64,2048]{1,0:T(8,128)}) %reduce-scatter.2.cloned.1.call-update) | async-done | bytes 524304 | tf_op jit(solution)/shard_map/reduce_scatter | solution.py:179
  (219 shorter events, 232.5 us)
Async XLA Ops:
  7.2 716.6 %reduce-scatter.2.cloned.1.call-start = ((), (), s32[]{:S(2)}) async-start(), calls=%async_computation.1 | async-start | bytes 4718592 | tf_op jit(solution)/shard_map/reduce_scatter | solution.py:179
  286.4 12.0 %collective-permute-start = (f32[4,128,128]{2,1,0:T(8,128)S(1)}, f32[4,128,128]{2,1,0:T(8,128)S(1)}, u32[]{:S(2)}, u32[]{:S(2)}) collective-permute-start(f32[4,128,128]{2,1,0:T(8,128)S(1)} %convolution_add_fusion.4), channel_id=1, source_target_pairs={{0,8},{8,16},{16,24},{24,32},{32,40},{40,48},{48,56},{56,64},{64,7... | collective-permute-start | bytes 786440 | tf_op jit(solution)/shard_map/while/body/eval_jaxpr/ppermute | solution.py:18
  298.9 11.2 %collective-permute-start = (f32[4,128,128]{2,1,0:T(8,128)S(1)}, f32[4,128,128]{2,1,0:T(8,128)S(1)}, u32[]{:S(2)}, u32[]{:S(2)}) collective-permute-start(f32[4,128,128]{2,1,0:T(8,128)S(1)} %convolution_add_fusion.4), channel_id=1, source_target_pairs={{0,8},{8,16},{16,24},{24,32},{32,40},{40,48},{48,56},{56,64},{64,7... | collective-permute-start | bytes 786440 | tf_op jit(solution)/shard_map/while/body/eval_jaxpr/ppermute | solution.py:18
  310.4 10.4 %collective-permute-start = (f32[4,128,128]{2,1,0:T(8,128)S(1)}, f32[4,128,128]{2,1,0:T(8,128)S(1)}, u32[]{:S(2)}, u32[]{:S(2)}) collective-permute-start(f32[4,128,128]{2,1,0:T(8,128)S(1)} %convolution_add_fusion.4), channel_id=1, source_target_pairs={{0,8},{8,16},{16,24},{24,32},{32,40},{40,48},{48,56},{56,64},{64,7... | collective-permute-start | bytes 786440 | tf_op jit(solution)/shard_map/while/body/eval_jaxpr/ppermute | solution.py:18
  321.2 10.4 %collective-permute-start = (f32[4,128,128]{2,1,0:T(8,128)S(1)}, f32[4,128,128]{2,1,0:T(8,128)S(1)}, u32[]{:S(2)}, u32[]{:S(2)}) collective-permute-start(f32[4,128,128]{2,1,0:T(8,128)S(1)} %convolution_add_fusion.4), channel_id=1, source_target_pairs={{0,8},{8,16},{16,24},{24,32},{32,40},{40,48},{48,56},{56,64},{64,7... | collective-permute-start | bytes 786440 | tf_op jit(solution)/shard_map/while/body/eval_jaxpr/ppermute | solution.py:18
  332.0 10.4 %collective-permute-start = (f32[4,128,128]{2,1,0:T(8,128)S(1)}, f32[4,128,128]{2,1,0:T(8,128)S(1)}, u32[]{:S(2)}, u32[]{:S(2)}) collective-permute-start(f32[4,128,128]{2,1,0:T(8,128)S(1)} %convolution_add_fusion.4), channel_id=1, source_target_pairs={{0,8},{8,16},{16,24},{24,32},{32,40},{40,48},{48,56},{56,64},{64,7... | collective-permute-start | bytes 786440 | tf_op jit(solution)/shard_map/while/body/eval_jaxpr/ppermute | solution.py:18
  342.8 10.4 %collective-permute-start = (f32[4,128,128]{2,1,0:T(8,128)S(1)}, f32[4,128,128]{2,1,0:T(8,128)S(1)}, u32[]{:S(2)}, u32[]{:S(2)}) collective-permute-start(f32[4,128,128]{2,1,0:T(8,128)S(1)} %convolution_add_fusion.4), channel_id=1, source_target_pairs={{0,8},{8,16},{16,24},{24,32},{32,40},{40,48},{48,56},{56,64},{64,7... | collective-permute-start | bytes 786440 | tf_op jit(solution)/shard_map/while/body/eval_jaxpr/ppermute | solution.py:18
  353.5 11.0 %collective-permute-start = (f32[4,128,128]{2,1,0:T(8,128)S(1)}, f32[4,128,128]{2,1,0:T(8,128)S(1)}, u32[]{:S(2)}, u32[]{:S(2)}) collective-permute-start(f32[4,128,128]{2,1,0:T(8,128)S(1)} %convolution_add_fusion.4), channel_id=1, source_target_pairs={{0,8},{8,16},{16,24},{24,32},{32,40},{40,48},{48,56},{56,64},{64,7... | collective-permute-start | bytes 786440 | tf_op jit(solution)/shard_map/while/body/eval_jaxpr/ppermute | solution.py:18
  365.0 12.2 %collective-permute-start = (f32[4,128,128]{2,1,0:T(8,128)S(1)}, f32[4,128,128]{2,1,0:T(8,128)S(1)}, u32[]{:S(2)}, u32[]{:S(2)}) collective-permute-start(f32[4,128,128]{2,1,0:T(8,128)S(1)} %convolution_add_fusion.4), channel_id=1, source_target_pairs={{0,8},{8,16},{16,24},{24,32},{32,40},{40,48},{48,56},{56,64},{64,7... | collective-permute-start | bytes 786440 | tf_op jit(solution)/shard_map/while/body/eval_jaxpr/ppermute | solution.py:18
  377.5 13.0 %collective-permute-start = (f32[4,128,128]{2,1,0:T(8,128)S(1)}, f32[4,128,128]{2,1,0:T(8,128)S(1)}, u32[]{:S(2)}, u32[]{:S(2)}) collective-permute-start(f32[4,128,128]{2,1,0:T(8,128)S(1)} %convolution_add_fusion.4), channel_id=1, source_target_pairs={{0,8},{8,16},{16,24},{24,32},{32,40},{40,48},{48,56},{56,64},{64,7... | collective-permute-start | bytes 786440 | tf_op jit(solution)/shard_map/while/body/eval_jaxpr/ppermute | solution.py:18
  391.0 12.2 %collective-permute-start = (f32[4,128,128]{2,1,0:T(8,128)S(1)}, f32[4,128,128]{2,1,0:T(8,128)S(1)}, u32[]{:S(2)}, u32[]{:S(2)}) collective-permute-start(f32[4,128,128]{2,1,0:T(8,128)S(1)} %convolution_add_fusion.4), channel_id=1, source_target_pairs={{0,8},{8,16},{16,24},{24,32},{32,40},{40,48},{48,56},{56,64},{64,7... | collective-permute-start | bytes 786440 | tf_op jit(solution)/shard_map/while/body/eval_jaxpr/ppermute | solution.py:18
  403.6 11.3 %collective-permute-start = (f32[4,128,128]{2,1,0:T(8,128)S(1)}, f32[4,128,128]{2,1,0:T(8,128)S(1)}, u32[]{:S(2)}, u32[]{:S(2)}) collective-permute-start(f32[4,128,128]{2,1,0:T(8,128)S(1)} %convolution_add_fusion.4), channel_id=1, source_target_pairs={{0,8},{8,16},{16,24},{24,32},{32,40},{40,48},{48,56},{56,64},{64,7... | collective-permute-start | bytes 786440 | tf_op jit(solution)/shard_map/while/body/eval_jaxpr/ppermute | solution.py:18
  415.3 10.4 %collective-permute-start = (f32[4,128,128]{2,1,0:T(8,128)S(1)}, f32[4,128,128]{2,1,0:T(8,128)S(1)}, u32[]{:S(2)}, u32[]{:S(2)}) collective-permute-start(f32[4,128,128]{2,1,0:T(8,128)S(1)} %convolution_add_fusion.4), channel_id=1, source_target_pairs={{0,8},{8,16},{16,24},{24,32},{32,40},{40,48},{48,56},{56,64},{64,7... | collective-permute-start | bytes 786440 | tf_op jit(solution)/shard_map/while/body/eval_jaxpr/ppermute | solution.py:18
  426.1 10.4 %collective-permute-start = (f32[4,128,128]{2,1,0:T(8,128)S(1)}, f32[4,128,128]{2,1,0:T(8,128)S(1)}, u32[]{:S(2)}, u32[]{:S(2)}) collective-permute-start(f32[4,128,128]{2,1,0:T(8,128)S(1)} %convolution_add_fusion.4), channel_id=1, source_target_pairs={{0,8},{8,16},{16,24},{24,32},{32,40},{40,48},{48,56},{56,64},{64,7... | collective-permute-start | bytes 786440 | tf_op jit(solution)/shard_map/while/body/eval_jaxpr/ppermute | solution.py:18
  436.9 10.4 %collective-permute-start = (f32[4,128,128]{2,1,0:T(8,128)S(1)}, f32[4,128,128]{2,1,0:T(8,128)S(1)}, u32[]{:S(2)}, u32[]{:S(2)}) collective-permute-start(f32[4,128,128]{2,1,0:T(8,128)S(1)} %convolution_add_fusion.4), channel_id=1, source_target_pairs={{0,8},{8,16},{16,24},{24,32},{32,40},{40,48},{48,56},{56,64},{64,7... | collective-permute-start | bytes 786440 | tf_op jit(solution)/shard_map/while/body/eval_jaxpr/ppermute | solution.py:18
  447.7 10.4 %collective-permute-start = (f32[4,128,128]{2,1,0:T(8,128)S(1)}, f32[4,128,128]{2,1,0:T(8,128)S(1)}, u32[]{:S(2)}, u32[]{:S(2)}) collective-permute-start(f32[4,128,128]{2,1,0:T(8,128)S(1)} %convolution_add_fusion.4), channel_id=1, source_target_pairs={{0,8},{8,16},{16,24},{24,32},{32,40},{40,48},{48,56},{56,64},{64,7... | collective-permute-start | bytes 786440 | tf_op jit(solution)/shard_map/while/body/eval_jaxpr/ppermute | solution.py:18
  458.4 10.9 %collective-permute-start = (f32[4,128,128]{2,1,0:T(8,128)S(1)}, f32[4,128,128]{2,1,0:T(8,128)S(1)}, u32[]{:S(2)}, u32[]{:S(2)}) collective-permute-start(f32[4,128,128]{2,1,0:T(8,128)S(1)} %convolution_add_fusion.4), channel_id=1, source_target_pairs={{0,8},{8,16},{16,24},{24,32},{32,40},{40,48},{48,56},{56,64},{64,7... | collective-permute-start | bytes 786440 | tf_op jit(solution)/shard_map/while/body/eval_jaxpr/ppermute | solution.py:18
  469.7 12.0 %collective-permute-start = (f32[4,128,128]{2,1,0:T(8,128)S(1)}, f32[4,128,128]{2,1,0:T(8,128)S(1)}, u32[]{:S(2)}, u32[]{:S(2)}) collective-permute-start(f32[4,128,128]{2,1,0:T(8,128)S(1)} %convolution_add_fusion.4), channel_id=1, source_target_pairs={{0,8},{8,16},{16,24},{24,32},{32,40},{40,48},{48,56},{56,64},{64,7... | collective-permute-start | bytes 786440 | tf_op jit(solution)/shard_map/while/body/eval_jaxpr/ppermute | solution.py:18
  482.2 13.2 %collective-permute-start = (f32[4,128,128]{2,1,0:T(8,128)S(1)}, f32[4,128,128]{2,1,0:T(8,128)S(1)}, u32[]{:S(2)}, u32[]{:S(2)}) collective-permute-start(f32[4,128,128]{2,1,0:T(8,128)S(1)} %convolution_add_fusion.4), channel_id=1, source_target_pairs={{0,8},{8,16},{16,24},{24,32},{32,40},{40,48},{48,56},{56,64},{64,7... | collective-permute-start | bytes 786440 | tf_op jit(solution)/shard_map/while/body/eval_jaxpr/ppermute | solution.py:18
  495.7 12.3 %collective-permute-start = (f32[4,128,128]{2,1,0:T(8,128)S(1)}, f32[4,128,128]{2,1,0:T(8,128)S(1)}, u32[]{:S(2)}, u32[]{:S(2)}) collective-permute-start(f32[4,128,128]{2,1,0:T(8,128)S(1)} %convolution_add_fusion.4), channel_id=1, source_target_pairs={{0,8},{8,16},{16,24},{24,32},{32,40},{40,48},{48,56},{56,64},{64,7... | collective-permute-start | bytes 786440 | tf_op jit(solution)/shard_map/while/body/eval_jaxpr/ppermute | solution.py:18
  508.5 11.5 %collective-permute-start = (f32[4,128,128]{2,1,0:T(8,128)S(1)}, f32[4,128,128]{2,1,0:T(8,128)S(1)}, u32[]{:S(2)}, u32[]{:S(2)}) collective-permute-start(f32[4,128,128]{2,1,0:T(8,128)S(1)} %convolution_add_fusion.4), channel_id=1, source_target_pairs={{0,8},{8,16},{16,24},{24,32},{32,40},{40,48},{48,56},{56,64},{64,7... | collective-permute-start | bytes 786440 | tf_op jit(solution)/shard_map/while/body/eval_jaxpr/ppermute | solution.py:18
  520.4 10.6 %collective-permute-start = (f32[4,128,128]{2,1,0:T(8,128)S(1)}, f32[4,128,128]{2,1,0:T(8,128)S(1)}, u32[]{:S(2)}, u32[]{:S(2)}) collective-permute-start(f32[4,128,128]{2,1,0:T(8,128)S(1)} %convolution_add_fusion.4), channel_id=1, source_target_pairs={{0,8},{8,16},{16,24},{24,32},{32,40},{40,48},{48,56},{56,64},{64,7... | collective-permute-start | bytes 786440 | tf_op jit(solution)/shard_map/while/body/eval_jaxpr/ppermute | solution.py:18
  531.3 10.4 %collective-permute-start = (f32[4,128,128]{2,1,0:T(8,128)S(1)}, f32[4,128,128]{2,1,0:T(8,128)S(1)}, u32[]{:S(2)}, u32[]{:S(2)}) collective-permute-start(f32[4,128,128]{2,1,0:T(8,128)S(1)} %convolution_add_fusion.4), channel_id=1, source_target_pairs={{0,8},{8,16},{16,24},{24,32},{32,40},{40,48},{48,56},{56,64},{64,7... | collective-permute-start | bytes 786440 | tf_op jit(solution)/shard_map/while/body/eval_jaxpr/ppermute | solution.py:18
  542.1 10.4 %collective-permute-start = (f32[4,128,128]{2,1,0:T(8,128)S(1)}, f32[4,128,128]{2,1,0:T(8,128)S(1)}, u32[]{:S(2)}, u32[]{:S(2)}) collective-permute-start(f32[4,128,128]{2,1,0:T(8,128)S(1)} %convolution_add_fusion.4), channel_id=1, source_target_pairs={{0,8},{8,16},{16,24},{24,32},{32,40},{40,48},{48,56},{56,64},{64,7... | collective-permute-start | bytes 786440 | tf_op jit(solution)/shard_map/while/body/eval_jaxpr/ppermute | solution.py:18
  552.9 10.4 %collective-permute-start = (f32[4,128,128]{2,1,0:T(8,128)S(1)}, f32[4,128,128]{2,1,0:T(8,128)S(1)}, u32[]{:S(2)}, u32[]{:S(2)}) collective-permute-start(f32[4,128,128]{2,1,0:T(8,128)S(1)} %convolution_add_fusion.4), channel_id=1, source_target_pairs={{0,8},{8,16},{16,24},{24,32},{32,40},{40,48},{48,56},{56,64},{64,7... | collective-permute-start | bytes 786440 | tf_op jit(solution)/shard_map/while/body/eval_jaxpr/ppermute | solution.py:18
  563.7 10.6 %collective-permute-start = (f32[4,128,128]{2,1,0:T(8,128)S(1)}, f32[4,128,128]{2,1,0:T(8,128)S(1)}, u32[]{:S(2)}, u32[]{:S(2)}) collective-permute-start(f32[4,128,128]{2,1,0:T(8,128)S(1)} %convolution_add_fusion.4), channel_id=1, source_target_pairs={{0,8},{8,16},{16,24},{24,32},{32,40},{40,48},{48,56},{56,64},{64,7... | collective-permute-start | bytes 786440 | tf_op jit(solution)/shard_map/while/body/eval_jaxpr/ppermute | solution.py:18
  574.6 12.1 %collective-permute-start = (f32[4,128,128]{2,1,0:T(8,128)S(1)}, f32[4,128,128]{2,1,0:T(8,128)S(1)}, u32[]{:S(2)}, u32[]{:S(2)}) collective-permute-start(f32[4,128,128]{2,1,0:T(8,128)S(1)} %convolution_add_fusion.4), channel_id=1, source_target_pairs={{0,8},{8,16},{16,24},{24,32},{32,40},{40,48},{48,56},{56,64},{64,7... | collective-permute-start | bytes 786440 | tf_op jit(solution)/shard_map/while/body/eval_jaxpr/ppermute | solution.py:18
  587.1 11.5 %collective-permute-start = (f32[4,128,128]{2,1,0:T(8,128)S(1)}, f32[4,128,128]{2,1,0:T(8,128)S(1)}, u32[]{:S(2)}, u32[]{:S(2)}) collective-permute-start(f32[4,128,128]{2,1,0:T(8,128)S(1)} %convolution_add_fusion.4), channel_id=1, source_target_pairs={{0,8},{8,16},{16,24},{24,32},{32,40},{40,48},{48,56},{56,64},{64,7... | collective-permute-start | bytes 786440 | tf_op jit(solution)/shard_map/while/body/eval_jaxpr/ppermute | solution.py:18
  599.1 10.5 %collective-permute-start = (f32[4,128,128]{2,1,0:T(8,128)S(1)}, f32[4,128,128]{2,1,0:T(8,128)S(1)}, u32[]{:S(2)}, u32[]{:S(2)}) collective-permute-start(f32[4,128,128]{2,1,0:T(8,128)S(1)} %convolution_add_fusion.4), channel_id=1, source_target_pairs={{0,8},{8,16},{16,24},{24,32},{32,40},{40,48},{48,56},{56,64},{64,7... | collective-permute-start | bytes 786440 | tf_op jit(solution)/shard_map/while/body/eval_jaxpr/ppermute | solution.py:18
  609.9 10.4 %collective-permute-start = (f32[4,128,128]{2,1,0:T(8,128)S(1)}, f32[4,128,128]{2,1,0:T(8,128)S(1)}, u32[]{:S(2)}, u32[]{:S(2)}) collective-permute-start(f32[4,128,128]{2,1,0:T(8,128)S(1)} %convolution_add_fusion.4), channel_id=1, source_target_pairs={{0,8},{8,16},{16,24},{24,32},{32,40},{40,48},{48,56},{56,64},{64,7... | collective-permute-start | bytes 786440 | tf_op jit(solution)/shard_map/while/body/eval_jaxpr/ppermute | solution.py:18
  620.7 10.6 %collective-permute-start = (f32[4,128,128]{2,1,0:T(8,128)S(1)}, f32[4,128,128]{2,1,0:T(8,128)S(1)}, u32[]{:S(2)}, u32[]{:S(2)}) collective-permute-start(f32[4,128,128]{2,1,0:T(8,128)S(1)} %convolution_add_fusion.4), channel_id=1, source_target_pairs={{0,8},{8,16},{16,24},{24,32},{32,40},{40,48},{48,56},{56,64},{64,7... | collective-permute-start | bytes 786440 | tf_op jit(solution)/shard_map/while/body/eval_jaxpr/ppermute | solution.py:18
  631.7 11.3 %collective-permute-start = (f32[4,128,128]{2,1,0:T(8,128)S(1)}, f32[4,128,128]{2,1,0:T(8,128)S(1)}, u32[]{:S(2)}, u32[]{:S(2)}) collective-permute-start(f32[4,128,128]{2,1,0:T(8,128)S(1)} %convolution_add_fusion.4), channel_id=1, source_target_pairs={{0,8},{8,16},{16,24},{24,32},{32,40},{40,48},{48,56},{56,64},{64,7... | collective-permute-start | bytes 786440 | tf_op jit(solution)/shard_map/while/body/eval_jaxpr/ppermute | solution.py:18
  (13 other events, 675.5 us)
Sparse Core Ops, SparseCore 0:
  652.8 71.0 reduce-scatter.1
where the time goes:
time: 740 us; the launch traced here: 735 us
  waiting for transfers between devices  353 us (48%)
  other arithmetic  172 us (23%)
  matrix products  118 us (16%)
  starting transfers between devices  61.1 us (8%)
  local copies, waits for them, and re-layouts  15.2 us (2%)
  between operations  14.3 us (2%)
    ppermute x31, waiting for transfers between devices, from_behind(): return lax.ppermute(x, axis, pairs)  283 us
    another operation x2, other arithmetic, block_pass(): jax.scipy.linalg.solve_triangular(system, right_side, lower=True, unit_di...  159 us
    dot_general x91, matrix products, product_matrix(): return jnp.einsum(pattern, first_op, second_op, precision=highest)  110 us
    reduce_scatter x1, waiting for transfers between devices, local(): lax.psum_scatter(jnp.dot(normed, out_weight, preferred_element_type=jnp.f...  70.2 us
    ppermute x31, starting transfers between devices, from_behind(): return lax.ppermute(x, axis, pairs)  61.1 us
  transfers between devices with their start and end apart: 32, of which 32 were waited for; matrix products, arithmetic and copies ran while one was open for 0% of the time, Pallas kernels for 0%

commit v1 on v0

v1 whole, which is shorter than its diff:
```python
import functools

import jax
import jax.numpy as jnp
from jax import lax
from jax.experimental import pallas as pl
from jax.experimental.pallas import tpu as pltpu
from jax.sharding import PartitionSpec as P

F32 = jnp.float32
BF16 = jnp.bfloat16
L = 128
EPS = 1e-6


def mm(a, b):
    return jnp.dot(a, b, preferred_element_type=F32)


def split(x):
    hi = x.astype(BF16)
    return hi, (x - hi.astype(F32)).astype(BF16)


def mm_wide(a, b):
    ah, al = split(a)
    bh, bl = split(b)
    row = jnp.concatenate([bh, bl], axis=1)
    r = mm(jnp.concatenate([ah, al], axis=1), jnp.concatenate([row, row], axis=0))
    n = b.shape[1]
    return r[:, :n] + r[:, n:]


def mm_three(a, b):
    ah, al = split(a)
    bh, bl = split(b)
    return mm(jnp.concatenate([ah, al, ah], axis=1), jnp.concatenate([bh, bh, bl], axis=0))


def mm_exact_right(a, b16):
    ah, al = split(a)
    return mm(jnp.concatenate([ah, al], axis=1), jnp.concatenate([b16, b16], axis=0))


def odd_rows(x, s):
    if s == 64:
        return x[64:]
    return jnp.concatenate([x[i : i + s] for i in range(s, L, 2 * s)], axis=0)


def weave(even, odd, s):
    parts = []
    for n, i in enumerate(range(0, L, 2 * s)):
        parts += [even[i : i + s], odd[n * s : (n + 1) * s]]
    return jnp.concatenate(parts, axis=0)


def unit_lower_inverse(systems):
    lane16 = lax.broadcasted_iota(jnp.int32, (16, L), 1)
    row16 = lax.broadcasted_iota(jnp.int32, (16, L), 0)
    place = lane16 // 16
    bands = []
    for a in systems:
        band = jnp.zeros((16, L), F32)
        for b in range(L // 16):
            band = jnp.where(place == b, a[16 * b : 16 * b + 16], band)
        bands.append(band)
    start = jnp.where(lane16 % 16 == row16, 1.0, 0.0).astype(F32)
    solved = [start for _ in systems]
    for m in range(15):
        index = place * 16 + m
        spread = [jnp.take_along_axis(band, index, axis=1) for band in bands]
        solved = [r - s * r[m : m + 1] for r, s in zip(solved, spread)]
    row = lax.broadcasted_iota(jnp.int32, (L, L), 0)
    lane = lax.broadcasted_iota(jnp.int32, (L, L), 1)
    same = row // 16 == lane // 16
    inverses = [jnp.where(same, jnp.concatenate([r] * (L // 16), axis=0), 0.0) for r in solved]
    for s in (16, 32, 64):
        below = odd_rows(row // s, s) == odd_rows(lane // s, s) + 1
        zeros = jnp.zeros((L, L), F32)
        lower = [mm_wide(jnp.where(below, odd_rows(a, s), 0.0), t) for a, t in zip(systems, inverses)]
        full = [weave(zeros, y, s) for y in lower]
        odd = [odd_rows(t, s) for t in inverses]
        change = [mm_wide(o, f) for o, f in zip(odd, full)]
        inverses = [weave(t, o - c, s) for t, o, c in zip(inverses, odd, change)]
    return inverses


def decay_columns(de_ref, bl_ref, dg_ref):
    row = lax.broadcasted_iota(jnp.int32, (8, 512), 0)
    lane = lax.broadcasted_iota(jnp.int32, (8, 512), 1) % L
    exponent = jnp.zeros((8, 512), jnp.int32)
    for h in range(4):
        exponent = jnp.where(row % 4 == h, de_ref[h], exponent)
    rate = jnp.exp2(exponent.astype(F32)) / 16384.0
    gate = jnp.concatenate([dg_ref[...]] * 2, axis=0)
    logit = jnp.concatenate([bl_ref[...]] * 2, axis=0)
    beta = jax.nn.sigmoid(logit)
    cum = -rate * gate
    for s in (1, 2, 4, 8, 16, 32, 64):
        cum = cum + jnp.where(lane >= s, pltpu.roll(cum, s, 1), 0.0)
    last = jnp.concatenate(
        [jnp.broadcast_to(cum[:, L * b + L - 1 : L * b + L], (8, L)) for b in range(4)], axis=1
    )
    growth = jnp.exp(cum)
    remain = jnp.exp(last - cum)
    final = jnp.exp(last)
    pieces = []
    for quantity in (cum, beta, growth, remain):
        pieces += [quantity[:, L * b : L * b + L] for b in range(4)]
    columns = jnp.concatenate(pieces, axis=0).T
    return cum, beta, growth, final, columns


def local_kernel(de_ref, q_ref, k_ref, v_ref, bl_ref, dg_ref, x_ref, out_ref, lead_s, pu_s, b_s, d_s):
    cum, beta, growth, final, columns = decay_columns(de_ref, bl_ref, dg_ref)

    def column(quantity, b, h):
        i = quantity * 32 + b * 8 + h
        return columns[:, i : i + 1]

    row = lax.broadcasted_iota(jnp.int32, (L, L), 0)
    lane = lax.broadcasted_iota(jnp.int32, (L, L), 1)
    strict = row > lane
    inclusive = row >= lane
    eye = jnp.where(row == lane, 1.0, 0.0).astype(F32)

    key_norm, query_norm = {}, {}
    table = jnp.zeros((L, L), F32)
    for b in range(4):
        for kh in range(2):
            key = k_ref[L * b : L * b + L, L * kh : L * kh + L].astype(F32)
            query = q_ref[L * b : L * b + L, L * kh : L * kh + L].astype(F32)
            rk = lax.rsqrt(jnp.sum(key * key, axis=1, keepdims=True) + EPS)
            rq = lax.rsqrt(jnp.sum(query * query, axis=1, keepdims=True) + EPS) * (L**-0.5)
            key_norm[b, kh], query_norm[b, kh] = rk, rq
            table = jnp.where(lane == 2 * b + kh, rk, table)
    key_rows = table.T

    for b in range(4):
        tokens = slice(L * b, L * b + L)
        systems, scores, keys, keys_t, queries, vals = [], [], [], [], [], []
        for kh in range(2):
            key = k_ref[tokens, L * kh : L * kh + L]
            query = q_ref[tokens, L * kh : L * kh + L]
            key_t = key.T
            gram = mm(jnp.concatenate([query, key], axis=0), key_t)
            rk, rq = key_norm[b, kh], query_norm[b, kh]
            rk_row = key_rows[2 * b + kh : 2 * b + kh + 1]
            qk = gram[:L] * rk_row
            kk = gram[L:] * rk_row
            for h in (2 * kh, 2 * kh + 1):
                cum_row = cum[h : h + 1, tokens]
                fade = jnp.exp(jnp.minimum(column(0, b, h) - cum_row, 0.0))
                systems.append(jnp.where(strict, kk * (rk * column(1, b, h)) * fade, 0.0))
                scores.append(jnp.where(inclusive, qk * rq * fade, 0.0))
                keys.append(key)
                keys_t.append(key_t)
                queries.append(query)
                vals.append(v_ref[tokens, L * h : L * h + L])
        inverses = unit_lower_inverse(systems)
        for h in range(4):
            rk_row = key_rows[2 * b + h // 2 : 2 * b + h // 2 + 1]
            rk, rq = key_norm[b, h // 2], query_norm[b, h // 2]
            t1 = inverses[h] * beta[h : h + 1, tokens]
            r1 = mm_wide(scores[h], t1)
            both = jnp.concatenate([t1, r1], axis=0)
            written = mm_exact_right(both, vals[h])
            widened = mm_exact_right(both * (growth[h : h + 1, tokens] * rk_row), keys[h])
            pu_s[4 * b + h] = written[L:]
            lead_s[4 * b + h] = queries[h].astype(F32) * (column(2, b, h) * rq) - widened[L:]
            rem = column(3, b, h) * rk
            wu = jnp.concatenate([written[:L] * rem, widened[:L] * rem], axis=1)
            wh, wl = split(wu)
            kt = keys_t[h]
            change = mm(jnp.concatenate([kt, kt], axis=1), jnp.concatenate([wh, wl], axis=0))
            d_s[4 * b + h] = change[:, :L]
            b_s[4 * b + h] = eye * final[h : h + 1, tokens] - change[:, L:]

    zero = jnp.zeros((L, L), F32)
    state = [jnp.concatenate([d_s[h], b_s[h]], axis=1) for h in range(4)]
    for h in range(4):
        out_ref[h, 0:L, :] = jnp.concatenate([pu_s[h], lead_s[h]], axis=1)
    for b in range(1, 4):
        for h in range(4):
            out_ref[h, L * b : L * b + L, :] = mm_three(lead_s[4 * b + h], state[h]) + jnp.concatenate(
                [pu_s[4 * b + h], zero], axis=1
            )
        state = [
            mm_three(b_s[4 * b + h], state[h]) + jnp.concatenate([d_s[4 * b + h], zero], axis=1)
            for h in range(4)
        ]
    for h in range(4):
        x_ref[h] = state[h]


def local_part(queries, key_vec, values, beta_logit, decay_gate, decay_exp):
    vm = pl.BlockSpec(memory_space=pltpu.VMEM)
    return pl.pallas_call(
        local_kernel,
        out_shape=(
            jax.ShapeDtypeStruct((4, L, 2 * L), F32),
            jax.ShapeDtypeStruct((4, 512, 2 * L), F32),
        ),
        in_specs=[pl.BlockSpec(memory_space=pltpu.SMEM)] + [vm] * 5,
        out_specs=(vm, vm),
        scratch_shapes=[pltpu.VMEM((16, L, L), F32)] * 4,
        compiler_params=pltpu.CompilerParams(vmem_limit_bytes=48 * 1024 * 1024),
    )(decay_exp, queries, key_vec, values, beta_logit, decay_gate)


MESH_Y = 4


def to_ctx(ctx):
    return {"ctx": ctx}


def to_head(head):
    return {"head": head}


def exchange_kernel(nz, x_ref, sin_ref, gath, zbox, total, prefix, acc, outbox, landed, s1, r1, s2, r2, s3, r3):
    me = lax.axis_index("ctx")
    z, y = me // MESH_Y, lax.rem(me, MESH_Y)
    in_group = [z * MESH_Y + lax.rem(y + d, MESH_Y) for d in range(1, MESH_Y)]

    barrier = pltpu.get_barrier_semaphore()
    for other in in_group:
        pl.semaphore_signal(barrier, inc=1, device_id=to_ctx(other), device_id_type=pl.DeviceIdType.MESH)
    for d in range(1, nz):
        other = lax.rem(z + d, nz) * MESH_Y + y
        pl.semaphore_signal(barrier, inc=1, device_id=to_ctx(other), device_id_type=pl.DeviceIdType.MESH)
    pl.semaphore_wait(barrier, MESH_Y - 1 + nz - 1)

    firsts = []
    for d in range(1, MESH_Y):
        copy = pltpu.make_async_remote_copy(
            src_ref=x_ref.at[lax.rem(y + d, MESH_Y)],
            dst_ref=gath.at[y],
            send_sem=s1.at[d - 1],
            recv_sem=r1.at[d - 1],
            device_id=to_ctx(in_group[d - 1]),
            device_id_type=pl.DeviceIdType.MESH,
        )
        copy.start()
        firsts.append(copy)
    gath[y] = x_ref[y]
    for copy in firsts:
        copy.wait_recv()

    zero = jnp.zeros((L, L), F32)
    state = gath[0]
    for j in range(1, MESH_Y):
        prefix[j - 1] = state
        now = gath[j]
        state = mm_three(now[:, L:], state) + jnp.concatenate([now[:, :L], zero], axis=1)
    total[...] = state

    def z_copy(d):
        return pltpu.make_async_remote_copy(
            src_ref=total,
            dst_ref=zbox.at[z],
            send_sem=s2.at[d - 1],
            recv_sem=r2.at[d - 1],
            device_id=to_ctx(lax.rem(z + d, nz) * MESH_Y + y),
            device_id_type=pl.DeviceIdType.MESH,
        )

    for d in range(1, nz):

        @pl.when(z + d < nz)
        def _():
            z_copy(d).start()

    acc[...] = jnp.zeros((L, 2 * L), F32)
    for d in range(1, nz):

        @pl.when(z - d >= 0)
        def _():
            z_copy(d).wait_recv()
            if d == 1:
                acc[...] = zbox[z - d]
            else:
                so_far = acc[...]
                acc[...] = mm_three(so_far[:, L:], zbox[z - d]) + jnp.concatenate([so_far[:, :L], zero], axis=1)

    incoming = acc[:, :L]
    outbox[0] = incoming
    for j in range(1, MESH_Y):
        before = prefix[j - 1]
        outbox[j] = before[:, :L] + mm_three(before[:, L:], incoming)
    lasts = []
    for d in range(1, MESH_Y):
        copy = pltpu.make_async_remote_copy(
            src_ref=outbox.at[lax.rem(y + d, MESH_Y)],
            dst_ref=landed.at[y],
            send_sem=s3.at[d - 1],
            recv_sem=r3.at[d - 1],
            device_id=to_ctx(in_group[d - 1]),
            device_id_type=pl.DeviceIdType.MESH,
        )
        copy.start()
        lasts.append(copy)
    landed[y] = outbox[y]
    for copy in lasts:
        copy.wait_recv()
    sin_ref[...] = landed[...]
    for copy in firsts + lasts:
        copy.wait_send()
    for d in range(1, nz):

        @pl.when(z + d < nz)
        def _():
            z_copy(d).wait_send()


def exchange(x, nz):
    vm = pl.BlockSpec(memory_space=pltpu.VMEM)
    square = (MESH_Y, L, L)
    return pl.pallas_call(
        functools.partial(exchange_kernel, nz),
        out_shape=jax.ShapeDtypeStruct(square, F32),
        in_specs=[vm],
        out_specs=vm,
        scratch_shapes=[
            pltpu.VMEM((MESH_Y, L, 2 * L), F32),
            pltpu.VMEM((nz, L, 2 * L), F32),
            pltpu.VMEM((L, 2 * L), F32),
            pltpu.VMEM((MESH_Y - 1, L, 2 * L), F32),
            pltpu.VMEM((L, 2 * L), F32),
            pltpu.VMEM(square, F32),
            pltpu.VMEM(square, F32),
        ]
        + [pltpu.SemaphoreType.DMA((MESH_Y - 1,))] * 2
        + [pltpu.SemaphoreType.DMA((nz - 1,))] * 2
        + [pltpu.SemaphoreType.DMA((MESH_Y - 1,))] * 2,
        compiler_params=pltpu.CompilerParams(
            collective_id=0, has_side_effects=True, vmem_limit_bytes=24 * 1024 * 1024
        ),
    )(x)


MESH_X = 4
ROWS = 64
WIDE = 2048
HALF = WIDE // 2


def project_kernel(
    out_ref, sin_ref, gate_ref, gain_ref, w_ref, router_ref, old_ref, lo_ref, div_ref,
    normed, own, cores, corebox, ring1, box1, ring2, box2, sc, rc, s1, r1, s2, r2,
):
    me = lax.axis_index("head")
    x, c = me // 2, lax.rem(me, 2)
    right = lax.rem(x + 1, MESH_X) * 2 + c
    left = lax.rem(x + MESH_X - 1, MESH_X) * 2 + c
    twin = x * 2 + 1 - c

    barrier = pltpu.get_barrier_semaphore()
    for other in (right, left, twin):
        pl.semaphore_signal(barrier, inc=1, device_id=to_head(other), device_id_type=pl.DeviceIdType.MESH)
    pl.semaphore_wait(barrier, 3)

    def send(src, dst, ssem, rsem, head):
        copy = pltpu.make_async_remote_copy(
            src_ref=src, dst_ref=dst, send_sem=ssem, recv_sem=rsem,
            device_id=to_head(head), device_id_type=pl.DeviceIdType.MESH,
        )
        copy.start()
        return copy

    order = [lax.rem(x + d, MESH_X) for d in (2, 1, 3, 0)]
    core_copies = []

    def block(i):
        rows = pl.ds(pl.multiple_of(order[i] * L, L), L)
        parts = []
        for h in range(4):
            o = out_ref[h, rows, :]
            attended = o[:, :L] + mm_three(o[:, L:], sin_ref[h])
            scale = lax.rsqrt(jnp.mean(attended * attended, axis=1, keepdims=True) + EPS)
            gate = gate_ref[rows, L * h : L * h + L].astype(F32)
            parts.append((attended * scale * gain_ref[...] * (gate / (1.0 + jnp.exp(-gate)))).astype(BF16))
        normed[...] = jnp.concatenate(parts, axis=1)
        mine = normed[pl.ds(pl.multiple_of(c * ROWS, ROWS), ROWS), :]
        other = normed[pl.ds(pl.multiple_of((1 - c) * ROWS, ROWS), ROWS), :]
        both = jnp.concatenate([mine, other], axis=0)
        for n in range(4):
            cols = slice(512 * n, 512 * n + 512)
            partial = mm(both, w_ref[:, cols])
            own[i, :, cols] = partial[:ROWS]
            cores[i, :, cols] = partial[ROWS:].astype(BF16)
        core_copies.append(send(cores.at[i], corebox.at[i], sc.at[i], rc.at[i], twin))

    def pair_sum(i):
        core_copies[i].wait_recv()
        return own[i] + corebox[i].astype(F32)

    block(0)
    block(1)
    total = pair_sum(0)
    ring1[0] = total[:, :HALF].astype(BF16)
    ring1[1] = total[:, HALF:].astype(BF16)
    first = [
        send(ring1.at[0], box1.at[0], s1.at[0], r1.at[0], right),
        send(ring1.at[1], box1.at[1], s1.at[1], r1.at[1], left),
    ]
    block(2)
    block(3)
    total = pair_sum(1)
    first[0].wait_recv()
    ring2[0, :, :HALF] = (total[:, :HALF] + box1[0].astype(F32)).astype(BF16)
    ring2[0, :, HALF:] = total[:, HALF:].astype(BF16)
    second = [send(ring2.at[0], box2.at[0], s2.at[0], r2.at[0], right)]
    total = pair_sum(2)
    first[1].wait_recv()
    ring2[1, :, :HALF] = total[:, :HALF].astype(BF16)
    ring2[1, :, HALF:] = (total[:, HALF:] + box1[1].astype(F32)).astype(BF16)
    second.append(send(ring2.at[1], box2.at[1], s2.at[1], r2.at[1], left))

    old_logit = old_ref[...].astype(F32) / 1024.0
    old_logp = old_logit - jnp.log(jnp.sum(jnp.exp(old_logit), axis=1, keepdims=True))
    old_prob = jnp.exp(old_logp)

    total = pair_sum(3)
    for copy in second:
        copy.wait_recv()
    layer_out = (total + box2[0].astype(F32) + box2[1].astype(F32)).astype(BF16)
    lo_ref[...] = layer_out
    new_logit = mm(layer_out, router_ref[...])
    new_logp = new_logit - jnp.log(jnp.sum(jnp.exp(new_logit), axis=1, keepdims=True))
    div = jnp.sum(old_prob * (old_logp - new_logp), axis=1, keepdims=True)
    div_ref[...] = jnp.broadcast_to(div, (ROWS, L)).T[0:1, :]
    for copy in core_copies + first + second:
        copy.wait_send()


def project(outs, sin, gate, gain, w, router, old):
    vm = pl.BlockSpec(memory_space=pltpu.VMEM)
    return pl.pallas_call(
        project_kernel,
        out_shape=(
            jax.ShapeDtypeStruct((ROWS, WIDE), BF16),
            jax.ShapeDtypeStruct((1, ROWS), F32),
        ),
        in_specs=[vm] * 7,
        out_specs=(vm, vm),
        scratch_shapes=[
            pltpu.VMEM((L, 512), BF16),
            pltpu.VMEM((4, ROWS, WIDE), F32),
            pltpu.VMEM((4, ROWS, WIDE), BF16),
            pltpu.VMEM((4, ROWS, WIDE), BF16),
            pltpu.VMEM((2, ROWS, HALF), BF16),
            pltpu.VMEM((2, ROWS, HALF), BF16),
            pltpu.VMEM((2, ROWS, WIDE), BF16),
            pltpu.VMEM((2, ROWS, WIDE), BF16),
            pltpu.SemaphoreType.DMA((4,)),
            pltpu.SemaphoreType.DMA((4,)),
            pltpu.SemaphoreType.DMA((2,)),
            pltpu.SemaphoreType.DMA((2,)),
            pltpu.SemaphoreType.DMA((2,)),
            pltpu.SemaphoreType.DMA((2,)),
        ],
        compiler_params=pltpu.CompilerParams(
            collective_id=1, has_side_effects=True, vmem_limit_bytes=40 * 1024 * 1024
        ),
    )(outs, sin, gate, gain, w, router, old)


def solution(mesh):
    nz = mesh.shape["ctx"] // MESH_Y

    def local(
        queries, key_vec, values, out_gate, beta_logit, decay_gate, decay_exp,
        norm_gain, out_weight, router_weight, old_scores,
    ):
        x, outs = local_part(queries, key_vec, values, beta_logit, decay_gate, decay_exp)
        sin = exchange(x, nz)
        layer_out, div = project(
            outs, sin, out_gate, norm_gain.reshape(1, L), out_weight, router_weight, old_scores
        )
        return layer_out, div.reshape(ROWS)

    placed = (
        P("ctx", "head"), P("ctx", "head"), P("ctx", "head"), P("ctx", "head"), P("head", "ctx"),
        P("head", "ctx"), P("head"), P(), P("head", None), P(), P(("ctx", "head"), None),
    )
    return jax.shard_map(
        local,
        mesh=mesh,
        in_specs=placed,
        out_specs=(P(("ctx", "head"), None), P(("ctx", "head"))),
        check_vma=False,
    )
```

time: 740 us -> 85.4 us (0.12)
  waiting for transfers between devices: 353 us -> 0 us
  other arithmetic: 172 us -> 0 us
  matrix products: 118 us -> 0 us
  Pallas kernels: 0 us -> 73.4 us
  starting transfers between devices: 61.1 us -> 0 us
  between operations: 14.3 us -> 0.7 us
    ppermute x31 -> x0, waiting for transfers between devices: 283 us -> none  [from_behind(): return lax.ppermute(x, axis, pairs)]
    another operation x5 -> x0, other arithmetic: 160 us -> none  [the longest x2 159 us: block_pass(): jax.scipy.linalg.solve_triangular(system, right_side, lower=True, unit_di...]
    dot_general x93 -> x0, matrix products: 116 us -> none  [the longest x91 110 us: product_matrix(): return jnp.einsum(pattern, first_op, second_op, precision=highest)]
    pallas_call x0 -> x3, Pallas kernels: none -> 73.4 us  [the longest x1 43.6 us: exchange(): pl.pallas_call(functools.partial(exchange_kernel, nz), out_shape=jax.Shap...]
    reduce_scatter x1 -> x0, waiting for transfers between devices: 70.2 us -> none  [local(): lax.psum_scatter(jnp.dot(normed, out_weight, preferred_element_type=jnp.f...]
    ppermute x31 -> x0, starting transfers between devices: 61.1 us -> none  [from_behind(): return lax.ppermute(x, axis, pairs)]
    unnamed x27 -> x24, local copies, waits for them, and re-layouts: 1.64 us -> 11 us
  transfers between devices with their start and end apart: 32 -> 0, of which waited for: 32 -> 0; matrix products, arithmetic and copies ran while one was open for 0% -> 0% of each run, Pallas kernels for 0% -> 0%
where the time goes in v1:
time: 85.4 us; the launch traced here: 85.1 us
  Pallas kernels  73.4 us (86%)
  local copies, waits for them, and re-layouts  11 us (13%)
    pallas_call x1, Pallas kernels, exchange(): pl.pallas_call(functools.partial(exchange_kernel, nz), out_shape=jax.Shap...  43.6 us
    pallas_call x1, Pallas kernels, project(): pl.pallas_call(project_kernel, out_shape=(jax.ShapeDtypeStruct((ROWS, WID...  18.3 us
    pallas_call x1, Pallas kernels, local_part(): pl.pallas_call(local_kernel, out_shape=(jax.ShapeDtypeStruct((4, L, 2 * L...  11.5 us
    unnamed x24, local copies, waits for them, and re-layouts  11 us

profile of v1, /device:TPU:192, one launch (start us, length us, event | category | flops | bytes accessed | tf_op | source)
XLA Modules:
  0.0 85.1 jit_solution(4813738619460832852)
XLA Ops:
  0.6 0.0 copy-start.2
  0.6 0.0 copy-start.3
  0.7 1.1 %copy-done.3 = bf16[512,512]{1,0:T(8,128)(2,1)S(1)} copy-done((bf16[512,512]{1,0:T(8,128)(2,1)S(1)}, bf16[512,512]{1,0:T(8,128)(2,1)}, u32[]{:S(2)}) %copy-start.3) | copy-done | bytes 524312
  1.7 0.0 copy-start.4
  1.7 0.9 %copy-done.4 = bf16[512,256]{1,0:T(8,128)(2,1)S(1)} copy-done((bf16[512,256]{1,0:T(8,128)(2,1)S(1)}, bf16[512,256]{1,0:T(8,128)(2,1)}, u32[]{:S(2)}) %copy-start.4) | copy-done | bytes 262168
  2.7 0.0 copy-start.5
  2.7 0.9 %copy-done.5 = bf16[512,256]{1,0:T(8,128)(2,1)S(1)} copy-done((bf16[512,256]{1,0:T(8,128)(2,1)S(1)}, bf16[512,256]{1,0:T(8,128)(2,1)}, u32[]{:S(2)}) %copy-start.5) | copy-done | bytes 262168
  3.6 0.0 copy-start.7
  3.6 0.7 copy-done.7
  4.3 0.0 copy-start.8
  4.3 0.7 copy-done.8
  5.0 0.0 copy-start.9
  5.0 0.7 copy-done.9
  5.7 11.5 %shard_map.122 = (f32[4,128,256]{2,1,0:T(8,128)S(1)}, f32[4,512,256]{2,1,0:T(8,128)S(1)}) custom-call(s32[4]{0:T(128)S(1)} %copy-done.9, bf16[512,256]{1,0:T(8,128)(2,1)S(1)} %copy-done.4, bf16[512,256]{1,0:T(8,128)(2,1)S(1)} %copy-done.5, bf16[512,512]{1,0:T(8,128)(2,1)S(1)} %copy-done.3, f32[4,512]{1,0:T(4,128)S(1)} %copy-done.7, f32[4,512]{1,0:T(4,128)S(1)} %copy-done.8), custom_call_target="tpu_custom_call" | custom-call | tf_op jit(solution)/shard_map/pallas_call | solution.py:199
  17.2 43.6 %shard_map.123.sin_ref = f32[4,128,128]{2,1,0:T(8,128)S(1)} custom-call(f32[4,128,256]{2,1,0:T(8,128)S(1)} %get-tuple-element.7.x_ref), custom_call_target="tpu_custom_call" | custom-call | tf_op jit(solution)/shard_map/pallas_call | solution.py:321
  60.8 0.0 copy-done.2
  60.8 0.0 copy-start
  60.8 1.6 %copy-done = bf16[512,2048]{1,0:T(8,128)(2,1)S(1)} copy-done((bf16[512,2048]{1,0:T(8,128)(2,1)S(1)}, bf16[512,2048]{1,0:T(8,128)(2,1)}, u32[]{:S(2)}) %copy-start) | copy-done | bytes 2097176
  62.4 0.0 copy-start.1
  62.4 1.6 %copy-done.1 = bf16[2048,512]{1,0:T(8,128)(2,1)S(1)} copy-done((bf16[2048,512]{1,0:T(8,128)(2,1)S(1)}, bf16[2048,512]{1,0:T(8,128)(2,1)}, u32[]{:S(2)}) %copy-start.1) | copy-done | bytes 2097176
  64.0 0.0 copy-start.6
  64.0 0.9 %copy-done.6 = s32[64,512]{1,0:T(8,128)S(1)} copy-done((s32[64,512]{1,0:T(8,128)S(1)}, s32[64,512]{1,0:T(8,128)}, u32[]{:S(2)}) %copy-start.6) | copy-done | bytes 131096
  64.9 0.0 copy-start.10
  64.9 0.7 copy-done.10
  65.5 18.3 %shard_map.124 = (bf16[64,2048]{1,0:T(8,128)(2,1)S(1)}, f32[1,64]{1,0:T(1,128)S(1)}) custom-call(f32[4,512,256]{2,1,0:T(8,128)S(1)} %get-tuple-element.6.out_ref, f32[4,128,128]{2,1,0:T(8,128)S(1)} %shard_map.123.sin_ref, bf16[512,512]{1,0:T(8,128)(2,1)S(1)} %copy-done.2, f32[1,128]{1,0:T(1,128)S(1)} %bitcast.2, bf16[512,2048]{1,0:T(8,128)(2,1)S(1)} %copy-done, ...), custom_call_target="tpu_custom_call" | custom-call | tf_op jit(solution)/shard_map/pallas_call | solution.py:441
  83.9 0.7 copy.15
  84.6 0.5 copy.16
Async XLA Ops:
  0.6 60.2 %copy-start.2 = (bf16[512,512]{1,0:T(8,128)(2,1)S(1)}, bf16[512,512]{1,0:T(8,128)(2,1)}, u32[]{:S(2)}) copy-start(bf16[512,512]{1,0:T(8,128)(2,1)} %gate_ref.1) | copy-start | bytes 1572868
  0.6 1.1 %copy-start.3 = (bf16[512,512]{1,0:T(8,128)(2,1)S(1)}, bf16[512,512]{1,0:T(8,128)(2,1)}, u32[]{:S(2)}) copy-start(bf16[512,512]{1,0:T(8,128)(2,1)} %v_ref.1) | copy-start | bytes 1572868
  1.7 0.9 %copy-start.4 = (bf16[512,256]{1,0:T(8,128)(2,1)S(1)}, bf16[512,256]{1,0:T(8,128)(2,1)}, u32[]{:S(2)}) copy-start(bf16[512,256]{1,0:T(8,128)(2,1)} %q_ref.1) | copy-start | bytes 786436
  2.7 0.9 %copy-start.5 = (bf16[512,256]{1,0:T(8,128)(2,1)S(1)}, bf16[512,256]{1,0:T(8,128)(2,1)}, u32[]{:S(2)}) copy-start(bf16[512,256]{1,0:T(8,128)(2,1)} %k_ref.1) | copy-start | bytes 786436
  3.6 0.7 copy-start.7
  4.3 0.7 copy-start.8
  5.0 0.7 copy-start.9
  60.8 1.6 %copy-start = (bf16[512,2048]{1,0:T(8,128)(2,1)S(1)}, bf16[512,2048]{1,0:T(8,128)(2,1)}, u32[]{:S(2)}) copy-start(bf16[512,2048]{1,0:T(8,128)(2,1)} %w_ref.1) | copy-start | bytes 6291460
  62.4 1.6 %copy-start.1 = (bf16[2048,512]{1,0:T(8,128)(2,1)S(1)}, bf16[2048,512]{1,0:T(8,128)(2,1)}, u32[]{:S(2)}) copy-start(bf16[2048,512]{1,0:T(8,128)(2,1)} %router_ref.1) | copy-start | bytes 6291460
  64.0 0.9 %copy-start.6 = (s32[64,512]{1,0:T(8,128)S(1)}, s32[64,512]{1,0:T(8,128)}, u32[]{:S(2)}) copy-start(s32[64,512]{1,0:T(8,128)} %old_ref.1) | copy-start | bytes 393220
  64.9 0.7 copy-start.10

commit v2 on v1

v2 whole, which is shorter than its diff:
```python
import functools

import jax
import jax.numpy as jnp
from jax import lax
from jax.experimental import pallas as pl
from jax.experimental.pallas import tpu as pltpu
from jax.sharding import PartitionSpec as P

F32 = jnp.float32
BF16 = jnp.bfloat16
L = 128
EPS = 1e-6


def mm(a, b):
    return jnp.dot(a, b, preferred_element_type=F32)


def split(x):
    hi = x.astype(BF16)
    return hi, (x - hi.astype(F32)).astype(BF16)


def mm_wide(a, b):
    ah, al = split(a)
    bh, bl = split(b)
    row = jnp.concatenate([bh, bl], axis=1)
    r = mm(jnp.concatenate([ah, al], axis=1), jnp.concatenate([row, row], axis=0))
    n = b.shape[1]
    return r[:, :n] + r[:, n:]


def mm_three(a, b):
    ah, al = split(a)
    bh, bl = split(b)
    return mm(jnp.concatenate([ah, al, ah], axis=1), jnp.concatenate([bh, bh, bl], axis=0))


def mm_exact_right(a, b16):
    ah, al = split(a)
    return mm(jnp.concatenate([ah, al], axis=1), jnp.concatenate([b16, b16], axis=0))


def odd_rows(x, s):
    if s == 64:
        return x[64:]
    return jnp.concatenate([x[i : i + s] for i in range(s, L, 2 * s)], axis=0)


def weave(even, odd, s):
    parts = []
    for n, i in enumerate(range(0, L, 2 * s)):
        parts += [even[i : i + s], odd[n * s : (n + 1) * s]]
    return jnp.concatenate(parts, axis=0)


def unit_lower_inverse(systems):
    lane16 = lax.broadcasted_iota(jnp.int32, (16, L), 1)
    row16 = lax.broadcasted_iota(jnp.int32, (16, L), 0)
    place = lane16 // 16
    bands = []
    for a in systems:
        band = jnp.zeros((16, L), F32)
        for b in range(L // 16):
            band = jnp.where(place == b, a[16 * b : 16 * b + 16], band)
        bands.append(band)
    start = jnp.where(lane16 % 16 == row16, 1.0, 0.0).astype(F32)
    solved = [start for _ in systems]
    for m in range(15):
        index = place * 16 + m
        spread = [jnp.take_along_axis(band, index, axis=1) for band in bands]
        solved = [r - s * r[m : m + 1] for r, s in zip(solved, spread)]
    row = lax.broadcasted_iota(jnp.int32, (L, L), 0)
    lane = lax.broadcasted_iota(jnp.int32, (L, L), 1)
    same = row // 16 == lane // 16
    inverses = [jnp.where(same, jnp.concatenate([r] * (L // 16), axis=0), 0.0) for r in solved]
    for s in (16, 32, 64):
        below = odd_rows(row // s, s) == odd_rows(lane // s, s) + 1
        zeros = jnp.zeros((L, L), F32)
        lower = [mm_wide(jnp.where(below, odd_rows(a, s), 0.0), t) for a, t in zip(systems, inverses)]
        full = [weave(zeros, y, s) for y in lower]
        odd = [odd_rows(t, s) for t in inverses]
        change = [mm_wide(o, f) for o, f in zip(odd, full)]
        inverses = [weave(t, o - c, s) for t, o, c in zip(inverses, odd, change)]
    return inverses


ROWS = 64
WIDE = 2048
HALF = WIDE // 2
MESH_X = 4
MESH_Y = 4
QUAD = 4
PACK = L + 16


def to_ctx(ctx):
    return {"ctx": ctx}


def to_head(head):
    return {"head": head}


def signal(semaphore, device):
    pl.semaphore_signal(semaphore, inc=1, device_id=device, device_id_type=pl.DeviceIdType.MESH)


def remote(src, dst, send_sem, recv_sem, device):
    return pltpu.make_async_remote_copy(
        src_ref=src, dst_ref=dst, send_sem=send_sem, recv_sem=recv_sem,
        device_id=device, device_id_type=pl.DeviceIdType.MESH,
    )


def iotas():
    return lax.broadcasted_iota(jnp.int32, (L, L), 0), lax.broadcasted_iota(jnp.int32, (L, L), 1)


def decay_tables(de_ref, bl_ref, dg_ref, rows_s, cols_s):
    row = lax.broadcasted_iota(jnp.int32, (8, 512), 0)
    lane = lax.broadcasted_iota(jnp.int32, (8, 512), 1) % L
    exponent = jnp.zeros((8, 512), jnp.int32)
    for h in range(4):
        exponent = jnp.where(row % 4 == h, de_ref[h], exponent)
    rate = jnp.exp2(exponent.astype(F32)) / 16384.0
    gate = jnp.concatenate([dg_ref[...]] * 2, axis=0)
    beta = jax.nn.sigmoid(jnp.concatenate([bl_ref[...]] * 2, axis=0))
    cum = -rate * gate
    for s in (1, 2, 4, 8, 16, 32, 64):
        cum = cum + jnp.where(lane >= s, pltpu.roll(cum, s, 1), 0.0)
    growth = jnp.exp(cum)
    for b in range(4):
        tokens = slice(L * b, L * b + L)
        now = cum[:, tokens]
        last = jnp.broadcast_to(now[:, L - 1 : L], (8, L))
        parts = [now, beta[:, tokens], growth[:, tokens]]
        rows_s[b] = jnp.concatenate(parts + [jnp.exp(last)], axis=0)
        padding = [jnp.zeros((L - 32, L), F32)]
        cols_s[b] = jnp.concatenate(parts + [jnp.exp(last - now)] + padding, axis=0).T


def solve_block(b, q_ref, k_ref, v_ref, rows_s, cols_s, t1_s, score_s, b_s, d_s):
    row, lane = iotas()
    tokens = pl.ds(pl.multiple_of(b * L, L), L)
    rows, columns = rows_s[b], cols_s[b]
    systems, keys, norms = [], [], []
    table = jnp.zeros((L, L), F32)
    for kh in range(2):
        key = k_ref[tokens, L * kh : L * kh + L]
        query = q_ref[tokens, L * kh : L * kh + L]
        key32, query32 = key.astype(F32), query.astype(F32)
        rk = lax.rsqrt(jnp.sum(key32 * key32, axis=1, keepdims=True) + EPS)
        rq = lax.rsqrt(jnp.sum(query32 * query32, axis=1, keepdims=True) + EPS) * (L**-0.5)
        table = jnp.where(lane == kh, rk, table)
        columns = jnp.where(lane == 32 + kh, rq, columns)
        norms.append((rk, rq))
        keys.append((key, query))
    cols_s[b] = columns
    key_rows = table.T
    for kh in range(2):
        key, query = keys[kh]
        rk, rq = norms[kh]
        rk_row = key_rows[kh : kh + 1]
        key_t = key.T
        gram = mm(jnp.concatenate([query, key], axis=0), key_t)
        qk, kk = gram[:L] * rk_row, gram[L:] * rk_row
        keys[kh] = (key, key_t)
        for h in (2 * kh, 2 * kh + 1):
            fade = jnp.exp(jnp.minimum(columns[:, h : h + 1] - rows[h : h + 1], 0.0))
            systems.append(jnp.where(row > lane, kk * (rk * columns[:, 8 + h : 9 + h]) * fade, 0.0))
            score_s[4 * b + h] = jnp.where(row >= lane, qk * rq * fade, 0.0)
    inverses = unit_lower_inverse(systems)
    eye = jnp.where(row == lane, 1.0, 0.0).astype(F32)
    for h in range(4):
        kh = h // 2
        key, key_t = keys[kh]
        t1 = inverses[h] * rows[8 + h : 9 + h]
        t1_s[4 * b + h] = t1
        reach = rows[16 + h : 17 + h] * key_rows[kh : kh + 1]
        rows_s[b, 4 + h : 5 + h] = reach
        written = mm_exact_right(t1, v_ref[tokens, L * h : L * h + L])
        widened = mm_exact_right(t1 * reach, key)
        rem = columns[:, 24 + h : 25 + h] * norms[kh][0]
        wh, wl = split(jnp.concatenate([written * rem, widened * rem], axis=1))
        change = mm(jnp.concatenate([key_t, key_t], axis=1), jnp.concatenate([wh, wl], axis=0))
        d_s[4 * b + h] = change[:, :L]
        b_s[4 * b + h] = eye * rows[24 + h : 25 + h] - change[:, L:]


def output_block(b, q_ref, k_ref, v_ref, rows_s, cols_s, t1_s, score_s, state_s, out_s):
    tokens = pl.ds(pl.multiple_of(b * L, L), L)
    rows, columns = rows_s[b], cols_s[b]
    zero = jnp.zeros((L, L), F32)
    for h in range(4):
        kh = h // 2
        r1 = mm_wide(score_s[4 * b + h], t1_s[4 * b + h])
        from_values = mm_exact_right(r1, v_ref[tokens, L * h : L * h + L])
        from_keys = mm_exact_right(r1 * rows[4 + h : 5 + h], k_ref[tokens, L * kh : L * kh + L])
        query = q_ref[tokens, L * kh : L * kh + L].astype(F32)
        lead = query * (columns[:, 16 + h : 17 + h] * columns[:, 32 + kh : 33 + kh]) - from_keys
        out_s[4 * b + h] = mm_three(lead, state_s[4 * b + h]) + jnp.concatenate([from_values, zero], axis=1)


def pack(state):
    row, lane = iotas()
    kept = state.astype(BF16)
    lost = state[:, L:] - kept[:, L:].astype(F32)
    lost = jnp.sum(jnp.where(row == lane, lost, 0.0), axis=0, keepdims=True)
    lost = jnp.broadcast_to(jnp.concatenate([jnp.zeros((1, L), F32), lost], axis=1), (PACK - L, 2 * L))
    return jnp.concatenate([kept, lost.astype(BF16)], axis=0)


def lost_diagonal(packed):
    row, lane = iotas()
    return jnp.where(row == lane, packed[L : L + 1, L:].astype(F32), 0.0)


def unpack(packed):
    state = packed[:L].astype(F32)
    return jnp.concatenate([state[:, :L], state[:, L:] + lost_diagonal(packed)], axis=1)


def after(packed, state):
    m = packed[:L, L:]
    hi, lo = split(state)
    lhs = jnp.concatenate([m, lost_diagonal(packed).astype(BF16), m], axis=1)
    moved = mm(lhs, jnp.concatenate([hi, hi, lo], axis=0))
    return moved + jnp.concatenate([packed[:L, :L].astype(F32), jnp.zeros((L, L), F32)], axis=1)


def before(state, packed):
    hi, lo = split(state[:, L:])
    lost = jnp.concatenate([jnp.zeros((L, L), F32), lost_diagonal(packed)], axis=1).astype(BF16)
    moved = mm(
        jnp.concatenate([hi, lo, hi], axis=1), jnp.concatenate([packed[:L], packed[:L], lost], axis=0)
    )
    return moved + jnp.concatenate([state[:, :L], jnp.zeros((L, L), F32)], axis=1)


def layer_kernel(
    nz,
    de_ref, gain_ref, q_hbm, k_hbm, v_hbm, bl_hbm, dg_hbm, gate_hbm, w_hbm, router_hbm, old_hbm,
    lo_ref, div_ref,
    q_ref, k_ref, v_ref, bl_ref, dg_ref, gate_ref, w_ref, router_ref, old_ref,
    rows_s, cols_s, t1_s, score_s, b_s, d_s, state_s, out_s,
    packs, gath, prefix, total, zbox, acc, first_half, start, outbox, landed,
    normed, own, cores, corebox, ring1, box1, ring2, box2,
    load, ys, yr, zs, zr, hs, hr, ls, lr, sc, rc, s1, r1, s2, r2,
):
    ctx = lax.axis_index("ctx")
    z, y = ctx // MESH_Y, lax.rem(ctx, MESH_Y)
    quad, zq = z // QUAD, lax.rem(z, QUAD)
    head = lax.axis_index("head")
    x, c = head // 2, lax.rem(head, 2)
    in_group = [to_ctx(z * MESH_Y + lax.rem(y + d, MESH_Y)) for d in range(1, MESH_Y)]
    right = to_head(lax.rem(x + 1, MESH_X) * 2 + c)
    left = to_head(lax.rem(x + MESH_X - 1, MESH_X) * 2 + c)
    twin = to_head(x * 2 + 1 - c)

    loads = [
        pltpu.make_async_copy(src, dst, load.at[i])
        for i, (src, dst) in enumerate(
            (
                (bl_hbm, bl_ref), (dg_hbm, dg_ref), (k_hbm, k_ref), (q_hbm, q_ref), (v_hbm, v_ref),
                (gate_hbm, gate_ref), (w_hbm, w_ref), (router_hbm, router_ref), (old_hbm, old_ref),
            )
        )
    ]
    for copy in loads:
        copy.start()

    barrier = pltpu.get_barrier_semaphore()
    for device in in_group + [right, left, twin]:
        signal(barrier, device)
    for d in range(1, QUAD):
        signal(barrier, to_ctx((quad * QUAD + lax.rem(zq + d, QUAD)) * MESH_Y + y))

    @pl.when(z == QUAD - 1)
    def _():
        for other in range(QUAD, nz):
            signal(barrier, to_ctx(other * MESH_Y + y))

    @pl.when(z >= QUAD)
    def _():
        signal(barrier, to_ctx((QUAD - 1) * MESH_Y + y))

    for copy in loads[:2]:
        copy.wait()
    decay_tables(de_ref, bl_ref, dg_ref, rows_s, cols_s)
    for copy in loads[2:5]:
        copy.wait()

    def solve(b, carry):
        solve_block(b, q_ref, k_ref, v_ref, rows_s, cols_s, t1_s, score_s, b_s, d_s)
        return carry

    lax.fori_loop(0, 4, solve, 0)

    row, lane = iotas()
    zero = jnp.zeros((L, L), F32)
    eye = jnp.where(row == lane, 1.0, 0.0).astype(F32)
    states = []
    for h in range(4):
        state_s[h] = jnp.concatenate([zero, eye], axis=1)
        states.append(jnp.concatenate([d_s[h], b_s[h]], axis=1))
    for b in range(1, 4):
        for h in range(4):
            state_s[4 * b + h] = states[h]
        states = [
            mm_three(b_s[4 * b + h], states[h]) + jnp.concatenate([d_s[4 * b + h], zero], axis=1)
            for h in range(4)
        ]
    for h in range(4):
        packs[h] = pack(states[h])

    peers = MESH_Y - 1 + 3 + QUAD - 1

    @pl.when(z < QUAD - 1)
    def _():
        pl.semaphore_wait(barrier, peers)

    @pl.when(z == QUAD - 1)
    def _():
        pl.semaphore_wait(barrier, peers + nz - QUAD)

    @pl.when(z >= QUAD)
    def _():
        pl.semaphore_wait(barrier, peers + 1)

    firsts = [
        remote(packs.at[lax.rem(y + d, MESH_Y)], gath.at[y], ys.at[d - 1], yr.at[d - 1], in_group[d - 1])
        for d in range(1, MESH_Y)
    ]
    for copy in firsts:
        copy.start()
    gath[y] = packs[y]

    def output(b, carry):
        output_block(b, q_ref, k_ref, v_ref, rows_s, cols_s, t1_s, score_s, state_s, out_s)
        return carry

    lax.fori_loop(0, 3, output, 0)

    for copy in firsts:
        copy.wait_recv()
    state = unpack(gath[0])
    for j in range(1, MESH_Y):
        prefix[j - 1] = state
        state = after(gath[j], state)
    total[...] = pack(state)

    def quad_copy(d):
        device = to_ctx((quad * QUAD + lax.rem(zq + d, QUAD)) * MESH_Y + y)
        return remote(total, zbox.at[zq], zs.at[d - 1], zr.at[d - 1], device)

    for d in range(1, QUAD):

        @pl.when(zq + d < QUAD)
        def _():
            quad_copy(d).start()

    output(3, 0)
    acc[...] = jnp.concatenate([zero, eye], axis=1)
    for d in range(1, QUAD):

        @pl.when(zq - d >= 0)
        def _():
            quad_copy(d).wait_recv()
            acc[...] = unpack(zbox[zq - 1]) if d == 1 else before(acc[...], zbox[zq - d])

    def half_copy(other):
        device = to_ctx(other * MESH_Y + y)
        return remote(first_half.at[0], first_half.at[1], hs.at[other - QUAD], hr.at[0], device)

    @pl.when(z == QUAD - 1)
    def _():
        ended = state[:, :L] + mm_three(state[:, L:], acc[:, :L])
        first_half[0] = ended.astype(BF16)
        for other in range(QUAD, nz):
            half_copy(other).start()

    start[...] = acc[:, :L]

    @pl.when(z >= QUAD)
    def _():
        half_copy(QUAD).wait_recv()
        start[...] = acc[:, :L] + mm_exact_right(acc[:, L:], first_half[1])

    incoming = start[...]
    outbox[0] = incoming.astype(BF16)
    for j in range(1, MESH_Y):
        outbox[j] = (prefix[j - 1, :, :L] + mm_three(prefix[j - 1, :, L:], incoming)).astype(BF16)
    lasts = [
        remote(outbox.at[lax.rem(y + d, MESH_Y)], landed.at[y], ls.at[d - 1], lr.at[d - 1], in_group[d - 1])
        for d in range(1, MESH_Y)
    ]
    for copy in lasts:
        copy.start()
    landed[y] = outbox[y]

    for copy in loads[5:]:
        copy.wait()
    old_logit = old_ref[...].astype(F32) / 1024.0
    old_logp = old_logit - jnp.log(jnp.sum(jnp.exp(old_logit), axis=1, keepdims=True))
    old_prob = jnp.exp(old_logp)
    old_part = jnp.sum(old_prob * old_logp, axis=1, keepdims=True)

    for copy in lasts:
        copy.wait_recv()

    order = [lax.rem(x + d, MESH_X) for d in (2, 1, 3, 0)]

    def send(src, dst, ssem, rsem, device):
        copy = remote(src, dst, ssem, rsem, device)
        copy.start()
        return copy

    core_copies = []

    def project(i):
        rows = pl.ds(pl.multiple_of(order[i] * L, L), L)
        parts = []
        for h in range(4):
            o = out_s[4 * order[i] + h]
            attended = o[:, :L] + mm_exact_right(o[:, L:], landed[h])
            scale = lax.rsqrt(jnp.mean(attended * attended, axis=1, keepdims=True) + EPS)
            gate = gate_ref[rows, L * h : L * h + L].astype(F32)
            parts.append((attended * scale * gain_ref[...] * (gate / (1.0 + jnp.exp(-gate)))).astype(BF16))
        normed[...] = jnp.concatenate(parts, axis=1)
        mine = normed[pl.ds(pl.multiple_of(c * ROWS, ROWS), ROWS), :]
        other = normed[pl.ds(pl.multiple_of((1 - c) * ROWS, ROWS), ROWS), :]
        both = jnp.concatenate([mine, other], axis=0)
        for n in range(4):
            cols = slice(512 * n, 512 * n + 512)
            partial = mm(both, w_ref[:, cols])
            own[i, :, cols] = partial[:ROWS]
            cores[i, :, cols] = partial[ROWS:].astype(BF16)
        core_copies.append(send(cores.at[i], corebox.at[i], sc.at[i], rc.at[i], twin))

    def pair_sum(i, cols):
        return own[i, :, cols] + corebox[i, :, cols].astype(F32)

    near, far = slice(0, HALF), slice(HALF, WIDE)
    ring = []
    project(0)
    project(1)
    core_copies[0].wait_recv()
    ring1[0] = pair_sum(0, near).astype(BF16)
    ring.append(send(ring1.at[0], box1.at[0], s1.at[0], r1.at[0], right))
    ring1[1] = pair_sum(0, far).astype(BF16)
    ring.append(send(ring1.at[1], box1.at[1], s1.at[1], r1.at[1], left))
    project(2)
    core_copies[1].wait_recv()
    ring2[0] = pair_sum(1, far).astype(BF16)
    ring.append(send(ring2.at[0], box2.at[0], s2.at[0], r2.at[0], right))
    core_copies[2].wait_recv()
    ring2[1] = pair_sum(2, near).astype(BF16)
    ring.append(send(ring2.at[1], box2.at[1], s2.at[1], r2.at[1], left))
    project(3)
    ring[0].wait_recv()
    ring2[2] = (pair_sum(1, near) + box1[0].astype(F32)).astype(BF16)
    ring.append(send(ring2.at[2], box2.at[2], s2.at[2], r2.at[2], right))
    ring[1].wait_recv()
    ring2[3] = (pair_sum(2, far) + box1[1].astype(F32)).astype(BF16)
    ring.append(send(ring2.at[3], box2.at[3], s2.at[3], r2.at[3], left))
    core_copies[3].wait_recv()
    for copy in ring[2:]:
        copy.wait_recv()
    out_near = (pair_sum(3, near) + box2[2].astype(F32) + box2[1].astype(F32)).astype(BF16)
    out_far = (pair_sum(3, far) + box2[0].astype(F32) + box2[3].astype(F32)).astype(BF16)
    lo_ref[:, near] = out_near
    lo_ref[:, far] = out_far
    new_logit = mm(out_near, router_ref[near]) + mm(out_far, router_ref[far])
    new_logp = new_logit - jnp.log(jnp.sum(jnp.exp(new_logit), axis=1, keepdims=True))
    div = old_part - jnp.sum(old_prob * new_logp, axis=1, keepdims=True)
    div_ref[...] = jnp.broadcast_to(div, (ROWS, L)).T[0:1, :]

    for copy in firsts + lasts + core_copies + ring:
        copy.wait_send()
    for d in range(1, QUAD):

        @pl.when(zq + d < QUAD)
        def _():
            quad_copy(d).wait_send()

    @pl.when(z == QUAD - 1)
    def _():
        for other in range(QUAD, nz):
            half_copy(other).wait_send()


def layer(nz, *arrays):
    vm = pl.BlockSpec(memory_space=pltpu.VMEM)
    square = (MESH_Y, L, L)
    many = pltpu.VMEM((16, L, L), F32)
    wide = pltpu.VMEM((16, L, 2 * L), F32)
    dma = pltpu.SemaphoreType.DMA
    return pl.pallas_call(
        functools.partial(layer_kernel, nz),
        out_shape=(
            jax.ShapeDtypeStruct((ROWS, WIDE), BF16),
            jax.ShapeDtypeStruct((1, ROWS), F32),
        ),
        in_specs=[pl.BlockSpec(memory_space=pltpu.SMEM), vm] + [pl.BlockSpec(memory_space=pl.ANY)] * 9,
        out_specs=(vm, vm),
        scratch_shapes=[
            pltpu.VMEM((512, 256), BF16),
            pltpu.VMEM((512, 256), BF16),
            pltpu.VMEM((512, 512), BF16),
            pltpu.VMEM((4, 512), F32),
            pltpu.VMEM((4, 512), F32),
            pltpu.VMEM((512, 512), BF16),
            pltpu.VMEM((512, WIDE), BF16),
            pltpu.VMEM((WIDE, 512), BF16),
            pltpu.VMEM((ROWS, 512), jnp.int32),
            pltpu.VMEM((4, 32, L), F32),
            pltpu.VMEM((4, L, L), F32),
            many, many, many, many, wide, wide,
            pltpu.VMEM((MESH_Y, PACK, 2 * L), BF16),
            pltpu.VMEM((MESH_Y, PACK, 2 * L), BF16),
            pltpu.VMEM((MESH_Y - 1, L, 2 * L), F32),
            pltpu.VMEM((PACK, 2 * L), BF16),
            pltpu.VMEM((QUAD, PACK, 2 * L), BF16),
            pltpu.VMEM((L, 2 * L), F32),
            pltpu.VMEM((2, L, L), BF16),
            pltpu.VMEM((L, L), F32),
            pltpu.VMEM(square, BF16),
            pltpu.VMEM(square, BF16),
            pltpu.VMEM((L, 512), BF16),
            pltpu.VMEM((4, ROWS, WIDE), F32),
            pltpu.VMEM((4, ROWS, WIDE), BF16),
            pltpu.VMEM((4, ROWS, WIDE), BF16),
            pltpu.VMEM((2, ROWS, HALF), BF16),
            pltpu.VMEM((2, ROWS, HALF), BF16),
            pltpu.VMEM((4, ROWS, HALF), BF16),
            pltpu.VMEM((4, ROWS, HALF), BF16),
            dma((9,)),
            dma((3,)), dma((3,)), dma((3,)), dma((3,)),
            dma((max(nz - QUAD, 1),)), dma((1,)),
            dma((3,)), dma((3,)),
            dma((4,)), dma((4,)), dma((2,)), dma((2,)), dma((4,)), dma((4,)),
        ],
        compiler_params=pltpu.CompilerParams(
            collective_id=0, has_side_effects=True, vmem_limit_bytes=56 * 1024 * 1024
        ),
    )(*arrays)


def solution(mesh):
    nz = mesh.shape["ctx"] // MESH_Y

    def local(
        queries, key_vec, values, out_gate, beta_logit, decay_gate, decay_exp,
        norm_gain, out_weight, router_weight, old_scores,
    ):
        layer_out, div = layer(
            nz, decay_exp, norm_gain.reshape(1, L), queries, key_vec, values, beta_logit, decay_gate,
            out_gate, out_weight, router_weight, old_scores,
        )
        return layer_out, div.reshape(ROWS)

    placed = (
        P("ctx", "head"), P("ctx", "head"), P("ctx", "head"), P("ctx", "head"), P("head", "ctx"),
        P("head", "ctx"), P("head"), P(), P("head", None), P(), P(("ctx", "head"), None),
    )
    return jax.shard_map(
        local,
        mesh=mesh,
        in_specs=placed,
        out_specs=(P(("ctx", "head"), None), P(("ctx", "head"))),
        check_vma=False,
    )
```

time: 85.4 us -> 55.1 us (0.65)
  Pallas kernels: 73.4 us -> 51.2 us
  local copies, waits for them, and re-layouts: 11 us -> 2.8 us
    pallas_call x3 -> x1, Pallas kernels: 73.4 us -> 51.2 us  [layer(): pl.pallas_call(functools.partial(layer_kernel, nz), out_shape=(jax.ShapeD...]
    unnamed x24 -> x2, local copies, waits for them, and re-layouts: 11 us -> 2.8 us
where the time goes in v2:
time: 55.1 us; the launch traced here: 54.6 us
  Pallas kernels  51.2 us (93%)
  local copies, waits for them, and re-layouts  2.8 us (5%)
  between operations  0.64 us (1%)
    pallas_call x1, Pallas kernels, layer(): pl.pallas_call(functools.partial(layer_kernel, nz), out_shape=(jax.ShapeD...  51.2 us
    unnamed x2, local copies, waits for them, and re-layouts  2.8 us

profile of v2, /device:TPU:192, one launch (start us, length us, event | category | flops | bytes accessed | tf_op | source)
XLA Modules:
  0.0 54.6 jit_solution(18249397366309496312)
XLA Ops:
  0.6 51.2 %shard_map.122 = (bf16[64,2048]{1,0:T(8,128)(2,1)}, f32[1,64]{1,0:T(1,128)}) custom-call(s32[4]{0:T(128)} %de_ref.1, f32[1,128]{1,0:T(1,128)} %bitcast.2, bf16[512,256]{1,0:T(8,128)(2,1)} %q_hbm.1, bf16[512,256]{1,0:T(8,128)(2,1)} %k_hbm.1, bf16[512,512]{1,0:T(8,128)(2,1)} %v_hbm.1, f32[4,512]{1,0:T(4,128)} %bl_hbm.1, f32[4,512]{1,0:T(4,128)} %dg_hbm.1, ...), custom_call_target="tpu_custom_call" | custom-call | tf_op jit(solution)/shard_map/pallas_call | solution.py:500
  51.8 1.7 %copy.15 = bf16[64,2048]{1,0:T(8,128)(2,1)} copy(bf16[64,2048]{1,0:T(8,128)(2,1)} %get-tuple-element.8) | data formatting | bytes 524288
  53.5 1.1 %copy.16 = f32[64]{0:T(128)} copy(f32[64]{0:T(128)} %bitcast.3) | data formatting | bytes 512

commit v3 on v2

v3 whole, which is shorter than its diff:
```python
import jax
import jax.numpy as jnp
from jax import lax
from jax.experimental import pallas as pl
from jax.experimental.pallas import tpu as pltpu
from jax.sharding import PartitionSpec as P

F32 = jnp.float32
BF16 = jnp.bfloat16
L = 128
EPS = 1e-6


def mm(a, b):
    return jnp.dot(a, b, preferred_element_type=F32)


def split(x):
    hi = x.astype(BF16)
    return hi, (x - hi.astype(F32)).astype(BF16)


def mm_wide(a, b):
    ah, al = split(a)
    bh, bl = split(b)
    row = jnp.concatenate([bh, bl], axis=1)
    r = mm(jnp.concatenate([ah, al], axis=1), jnp.concatenate([row, row], axis=0))
    n = b.shape[1]
    return r[:, :n] + r[:, n:]


def mm_rows(a, b):
    n, wide = a.shape[0], b.shape[1]
    r = mm(jnp.concatenate(split(a), axis=0), jnp.concatenate(split(b), axis=1))
    return r[:n, :wide] + (r[:n, wide:] + r[n:, :wide])


def mm_three(a, b):
    ah, al = split(a)
    bh, bl = split(b)
    return mm(jnp.concatenate([ah, al, ah], axis=1), jnp.concatenate([bh, bh, bl], axis=0))


def mm_exact_right(a, b16):
    ah, al = split(a)
    return mm(jnp.concatenate([ah, al], axis=1), jnp.concatenate([b16, b16], axis=0))


def odd_rows(x, s):
    if s == 64:
        return x[64:]
    return jnp.concatenate([x[i : i + s] for i in range(s, L, 2 * s)], axis=0)


def weave(even, odd, s):
    parts = []
    for n, i in enumerate(range(0, L, 2 * s)):
        parts += [even[i : i + s], odd[n * s : (n + 1) * s]]
    return jnp.concatenate(parts, axis=0)


def unit_lower_inverse(systems):
    lane16 = lax.broadcasted_iota(jnp.int32, (16, L), 1)
    row16 = lax.broadcasted_iota(jnp.int32, (16, L), 0)
    place = lane16 // 16
    bands = []
    for a in systems:
        band = jnp.zeros((16, L), F32)
        for b in range(L // 16):
            band = jnp.where(place == b, a[16 * b : 16 * b + 16], band)
        bands.append(band)
    start = jnp.where(lane16 % 16 == row16, 1.0, 0.0).astype(F32)
    solved = [start for _ in systems]
    for m in range(15):
        index = place * 16 + m
        spread = [jnp.take_along_axis(band, index, axis=1) for band in bands]
        solved = [r - s * r[m : m + 1] for r, s in zip(solved, spread)]
    row = lax.broadcasted_iota(jnp.int32, (L, L), 0)
    lane = lax.broadcasted_iota(jnp.int32, (L, L), 1)
    same = row // 16 == lane // 16
    inverses = [jnp.where(same, jnp.concatenate([r] * (L // 16), axis=0), 0.0) for r in solved]
    for s in (16, 32, 64):
        below = odd_rows(row // s, s) == odd_rows(lane // s, s) + 1
        zeros = jnp.zeros((L, L), F32)
        lower = [mm_rows(jnp.where(below, odd_rows(a, s), 0.0), t) for a, t in zip(systems, inverses)]
        full = [weave(zeros, y, s) for y in lower]
        odd = [odd_rows(t, s) for t in inverses]
        change = [mm_rows(o, f) for o, f in zip(odd, full)]
        inverses = [weave(t, o - c, s) for t, o, c in zip(inverses, odd, change)]
    return inverses


ROWS = 64
WIDE = 2048
HALF = WIDE // 2
MESH_X = 4
MESH_Y = 4
QUAD = 4
PACK = L + 16


def to_ctx(ctx):
    return {"ctx": ctx}


def to_head(head):
    return {"head": head}


def signal(semaphore, device):
    pl.semaphore_signal(semaphore, inc=1, device_id=device, device_id_type=pl.DeviceIdType.MESH)


def remote(src, dst, send_sem, recv_sem, device):
    return pltpu.make_async_remote_copy(
        src_ref=src, dst_ref=dst, send_sem=send_sem, recv_sem=recv_sem,
        device_id=device, device_id_type=pl.DeviceIdType.MESH,
    )


def iotas():
    return lax.broadcasted_iota(jnp.int32, (L, L), 0), lax.broadcasted_iota(jnp.int32, (L, L), 1)


def decay_tables(de_ref, bl_ref, dg_ref, rows_s, cols_s):
    row = lax.broadcasted_iota(jnp.int32, (8, 512), 0)
    lane = lax.broadcasted_iota(jnp.int32, (8, 512), 1) % L
    exponent = jnp.zeros((8, 512), jnp.int32)
    for h in range(4):
        exponent = jnp.where(row % 4 == h, de_ref[h], exponent)
    rate = jnp.exp2(exponent.astype(F32)) / 16384.0
    gate = jnp.concatenate([dg_ref[...]] * 2, axis=0)
    beta = jax.nn.sigmoid(jnp.concatenate([bl_ref[...]] * 2, axis=0))
    cum = -rate * gate
    for s in (1, 2, 4, 8, 16, 32, 64):
        cum = cum + jnp.where(lane >= s, pltpu.roll(cum, s, 1), 0.0)
    growth = jnp.exp(cum)
    for b in range(4):
        tokens = slice(L * b, L * b + L)
        now = cum[:, tokens]
        last = jnp.broadcast_to(now[:, L - 1 : L], (8, L))
        parts = [now, beta[:, tokens], growth[:, tokens]]
        rows_s[b] = jnp.concatenate(parts + [jnp.exp(last)], axis=0)
        padding = [jnp.zeros((L - 32, L), F32)]
        cols_s[b] = jnp.concatenate(parts + [jnp.exp(last - now)] + padding, axis=0).T


def solve_blocks(blocks, q_ref, k_ref, v_ref, rows_s, cols_s, t1_s, fade_s, b_s, d_s):
    row, lane = iotas()
    eye = jnp.where(row == lane, 1.0, 0.0).astype(F32)
    tokens = [pl.ds(pl.multiple_of(b * L, L), L) for b in blocks]
    rows = [rows_s[b] for b in blocks]
    columns = [cols_s[b] for b in blocks]
    places = [(n, kh) for n in range(len(blocks)) for kh in range(2)]
    keys = [k_ref[tokens[n], L * kh : L * kh + L] for n, kh in places]
    keys_t = [key.T for key in keys]
    norms = [
        lax.rsqrt(jnp.sum(key.astype(F32) * key.astype(F32), axis=1, keepdims=True) + EPS) for key in keys
    ]
    grams = [mm(key, key_t) for key, key_t in zip(keys, keys_t)]
    key_rows = []
    for n, b in enumerate(blocks):
        table = jnp.where(lane == 0, norms[2 * n], jnp.where(lane == 1, norms[2 * n + 1], 0.0))
        key_rows.append(table.T)
        rows_s[b, 28:30] = key_rows[n][:2]
    spots = [(n, h) for n in range(len(blocks)) for h in range(4)]
    systems = []
    for n, h in spots:
        kh = h // 2
        fade = jnp.exp(jnp.minimum(columns[n][:, h : h + 1] - rows[n][h : h + 1], 0.0))
        fade = fade * key_rows[n][kh : kh + 1]
        fade_s[4 * blocks[n] + h] = fade
        scaled = grams[2 * n + kh] * (norms[2 * n + kh] * columns[n][:, 8 + h : 9 + h])
        systems.append(jnp.where(row > lane, scaled * fade, 0.0))
    inverses = unit_lower_inverse(systems)
    t1s = [t * rows[n][8 + h : 9 + h] for t, (n, h) in zip(inverses, spots)]
    reaches = [rows[n][16 + h : 17 + h] * key_rows[n][h // 2 : h // 2 + 1] for n, h in spots]
    for (n, h), t1, reach in zip(spots, t1s, reaches):
        t1_s[4 * blocks[n] + h] = t1
        rows_s[blocks[n], 4 + h : 5 + h] = reach
    written = [mm_exact_right(t1, v_ref[tokens[n], L * h : L * h + L]) for t1, (n, h) in zip(t1s, spots)]
    widened = [
        mm_exact_right(t1 * reach, keys[2 * n + h // 2]) for t1, reach, (n, h) in zip(t1s, reaches, spots)
    ]
    changes = []
    for (n, h), u, w in zip(spots, written, widened):
        rem = columns[n][:, 24 + h : 25 + h] * norms[2 * n + h // 2]
        wh, wl = split(jnp.concatenate([u * rem, w * rem], axis=1))
        kt = keys_t[2 * n + h // 2]
        changes.append(mm(jnp.concatenate([kt, kt], axis=1), jnp.concatenate([wh, wl], axis=0)))
    for (n, h), change in zip(spots, changes):
        d_s[4 * blocks[n] + h] = change[:, :L]
        b_s[4 * blocks[n] + h] = eye * rows[n][24 + h : 25 + h] - change[:, L:]


def output_block(b, q_ref, k_ref, v_ref, rows_s, cols_s, t1_s, fade_s, state_s, out_s):
    row, lane = iotas()
    tokens = pl.ds(pl.multiple_of(b * L, L), L)
    rows, columns = rows_s[b], cols_s[b]
    zero = jnp.zeros((L, L), F32)
    keys, queries, scales, grams = [], [], [], []
    for kh in range(2):
        key = k_ref[tokens, L * kh : L * kh + L]
        query = q_ref[tokens, L * kh : L * kh + L]
        query32 = query.astype(F32)
        scales.append(lax.rsqrt(jnp.sum(query32 * query32, axis=1, keepdims=True) + EPS) * (L**-0.5))
        grams.append(mm(query, key.T))
        keys.append(key)
        queries.append(query32)
    scores = [
        jnp.where(row >= lane, grams[h // 2] * scales[h // 2] * fade_s[4 * b + h], 0.0) for h in range(4)
    ]
    reads = [mm_wide(score, t1_s[4 * b + h]) for h, score in enumerate(scores)]
    from_values = [mm_exact_right(r, v_ref[tokens, L * h : L * h + L]) for h, r in enumerate(reads)]
    from_keys = [mm_exact_right(r * rows[4 + h : 5 + h], keys[h // 2]) for h, r in enumerate(reads)]
    for h in range(4):
        lead = queries[h // 2] * (columns[:, 16 + h : 17 + h] * scales[h // 2]) - from_keys[h]
        out_s[4 * b + h] = mm_three(lead, state_s[4 * b + h]) + jnp.concatenate([from_values[h], zero], axis=1)


def pack(state):
    row, lane = iotas()
    kept = state.astype(BF16)
    lost = state[:, L:] - kept[:, L:].astype(F32)
    lost = jnp.sum(jnp.where(row == lane, lost, 0.0), axis=0, keepdims=True)
    lost = jnp.broadcast_to(jnp.concatenate([jnp.zeros((1, L), F32), lost], axis=1), (PACK - L, 2 * L))
    return jnp.concatenate([kept, lost.astype(BF16)], axis=0)


def lost_diagonal(packed):
    row, lane = iotas()
    return jnp.where(row == lane, packed[L : L + 1, L:].astype(F32), 0.0)


def unpack(packed):
    state = packed[:L].astype(F32)
    return jnp.concatenate([state[:, :L], state[:, L:] + lost_diagonal(packed)], axis=1)


def after(packed, state):
    m = packed[:L, L:]
    hi, lo = split(state)
    lhs = jnp.concatenate([m, lost_diagonal(packed).astype(BF16), m], axis=1)
    moved = mm(lhs, jnp.concatenate([hi, hi, lo], axis=0))
    return moved + jnp.concatenate([packed[:L, :L].astype(F32), jnp.zeros((L, L), F32)], axis=1)


def after_state(packed, state):
    m = packed[:L, L:]
    hi, lo = split(state)
    lhs = jnp.concatenate([m, lost_diagonal(packed).astype(BF16), m], axis=1)
    return mm(lhs, jnp.concatenate([hi, hi, lo], axis=0)) + packed[:L, :L].astype(F32)


def before(state, packed):
    hi, lo = split(state[:, L:])
    lost = jnp.concatenate([jnp.zeros((L, L), F32), lost_diagonal(packed)], axis=1).astype(BF16)
    moved = mm(
        jnp.concatenate([hi, lo, hi], axis=1), jnp.concatenate([packed[:L], packed[:L], lost], axis=0)
    )
    return moved + jnp.concatenate([state[:, :L], jnp.zeros((L, L), F32)], axis=1)


def layer_kernel(
    de_hbm, gain_hbm, q_hbm, k_hbm, v_hbm, bl_hbm, dg_hbm, gate_hbm, w_hbm, router_hbm, old_hbm,
    lo_ref, div_ref,
    de_ref, gain_ref, q_ref, k_ref, v_ref, bl_ref, dg_ref, gate_ref, w_ref, w2_ref, router_ref, old_ref,
    rows_s, cols_s, t1_s, fade_s, b_s, d_s, state_s, out_s,
    packs, gath, prefix, total, zbox, acc, first_half, start, outbox, landed,
    normed, nbox, own, ring1, box1, ring2, box2,
    load, ys, yr, zs, zr, hs, hr, ls, lr, ws, wr, sc, rc, s1, r1, s2, r2,
):
    ctx = lax.axis_index("ctx")
    z, y = ctx // MESH_Y, lax.rem(ctx, MESH_Y)
    quad, zq = z // QUAD, lax.rem(z, QUAD)
    head = lax.axis_index("head")
    x, c = head // 2, lax.rem(head, 2)
    in_group = [to_ctx(z * MESH_Y + lax.rem(y + d, MESH_Y)) for d in range(1, MESH_Y)]
    right = to_head(lax.rem(x + 1, MESH_X) * 2 + c)
    left = to_head(lax.rem(x + MESH_X - 1, MESH_X) * 2 + c)
    twin = to_head(x * 2 + 1 - c)

    def at_z(other):
        return to_ctx(other * MESH_Y + y)

    loads = [
        pltpu.make_async_copy(src, dst, load.at[i])
        for i, (src, dst) in enumerate(
            (
                (de_hbm, de_ref), (bl_hbm, bl_ref), (dg_hbm, dg_ref), (k_hbm, k_ref), (v_hbm, v_ref),
                (q_hbm, q_ref), (w_hbm, w_ref), (gate_hbm, gate_ref), (gain_hbm, gain_ref),
                (router_hbm, router_ref), (old_hbm, old_ref),
            )
        )
    ]
    for copy in loads:
        copy.start()

    barrier = pltpu.get_barrier_semaphore()
    for device in in_group + [right, left, twin]:
        signal(barrier, device)
    for d in range(1, QUAD):
        signal(barrier, at_z(quad * QUAD + lax.rem(zq + d, QUAD)))
    serves = ((QUAD - 1, (QUAD, QUAD + 1)), (0, (2 * QUAD - 1, 2 * QUAD - 2)))
    for end, served in serves:

        @pl.when(z == end)
        def _():
            for other in served:
                signal(barrier, at_z(other))

        for other in served:

            @pl.when(z == other)
            def _():
                signal(barrier, at_z(end))

    for copy in loads[:3]:
        copy.wait()
    decay_tables(de_ref, bl_ref, dg_ref, rows_s, cols_s)
    for copy in loads[3:5]:
        copy.wait()
    solve_blocks(range(4), q_ref, k_ref, v_ref, rows_s, cols_s, t1_s, fade_s, b_s, d_s)

    row, lane = iotas()
    zero = jnp.zeros((L, L), F32)
    eye = jnp.where(row == lane, 1.0, 0.0).astype(F32)
    states = []
    for h in range(4):
        state_s[h] = jnp.concatenate([zero, eye], axis=1)
        states.append(jnp.concatenate([d_s[h], b_s[h]], axis=1))
    for b in range(1, 4):
        for h in range(4):
            state_s[4 * b + h] = states[h]
        states = [
            mm_three(b_s[4 * b + h], states[h]) + jnp.concatenate([d_s[4 * b + h], zero], axis=1)
            for h in range(4)
        ]
    for h, packed in enumerate([pack(state) for state in states]):
        packs[h] = packed

    peers = MESH_Y - 1 + 3 + QUAD - 1

    @pl.when(jnp.logical_or(z == 0, z == QUAD - 1))
    def _():
        pl.semaphore_wait(barrier, peers + 2)

    @pl.when(jnp.logical_and(z > 0, z < QUAD - 1))
    def _():
        pl.semaphore_wait(barrier, peers)

    @pl.when(z >= QUAD)
    def _():
        pl.semaphore_wait(barrier, peers + 1)

    firsts = [
        remote(packs.at[lax.rem(y + d, MESH_Y)], gath.at[y], ys.at[d - 1], yr.at[d - 1], in_group[d - 1])
        for d in range(1, MESH_Y)
    ]
    for copy in firsts:
        copy.start()
    gath[y] = packs[y]
    loads[6].wait()
    weights = remote(w_ref, w2_ref, ws.at[0], wr.at[0], twin)
    weights.start()
    loads[5].wait()

    def output(b, carry):
        output_block(b, q_ref, k_ref, v_ref, rows_s, cols_s, t1_s, fade_s, state_s, out_s)
        return carry

    lax.fori_loop(0, 4, output, 0)

    for copy in firsts:
        copy.wait_recv()
    state = unpack(gath[0])
    for j in range(1, MESH_Y):
        prefix[j - 1] = state
        state = after(gath[j], state)
    total[...] = pack(state)

    def up_copy(d):
        device = at_z(quad * QUAD + lax.rem(zq + d, QUAD))
        return remote(total, zbox.at[zq], zs.at[d - 1], zr.at[d - 1], device)

    def down_copy(d):
        return remote(total, zbox.at[zq], zs.at[QUAD - 1], zr.at[QUAD - 2 + d], at_z(0))

    for d in range(1, QUAD):

        @pl.when(zq + d < QUAD)
        def _():
            up_copy(d).start()

        @pl.when(z == d)
        def _():
            down_copy(d).start()

    for copy in loads[7:]:
        copy.wait()
    old_logit = old_ref[...].astype(F32) / 1024.0
    old_logp = old_logit - jnp.log(jnp.sum(jnp.exp(old_logit), axis=1, keepdims=True))
    old_prob = jnp.exp(old_logp)
    old_part = jnp.sum(old_prob * old_logp, axis=1, keepdims=True)

    acc[...] = jnp.concatenate([zero, eye], axis=1)
    for d in range(1, QUAD):

        @pl.when(zq - d >= 0)
        def _():
            up_copy(d).wait_recv()
            acc[...] = unpack(zbox[zq - 1]) if d == 1 else before(acc[...], zbox[zq - d])

    def half_copy(i, other):
        return remote(first_half.at[0], first_half.at[1], hs.at[i], hr.at[0], at_z(other))

    @pl.when(z == QUAD - 1)
    def _():
        ended = state[:, :L] + mm_three(state[:, L:], acc[:, :L])
        first_half[0] = ended.astype(BF16)
        for i, other in enumerate(serves[0][1]):
            half_copy(i, other).start()

    @pl.when(z == 0)
    def _():
        ended = state[:, :L]
        for d in range(1, QUAD):
            down_copy(d).wait_recv()
            ended = after_state(zbox[d], ended)
        first_half[0] = ended.astype(BF16)
        for i, other in enumerate(serves[1][1]):
            half_copy(i, other).start()

    start[...] = acc[:, :L]

    @pl.when(z >= QUAD)
    def _():
        half_copy(0, QUAD).wait_recv()
        start[...] = acc[:, :L] + mm_exact_right(acc[:, L:], first_half[1])

    incoming = start[...]
    outbox[0] = incoming.astype(BF16)
    moved = mm_three(jnp.concatenate([prefix[j, :, L:] for j in range(MESH_Y - 1)], axis=0), incoming)
    for j in range(1, MESH_Y):
        outbox[j] = (prefix[j - 1, :, :L] + moved[L * (j - 1) : L * j]).astype(BF16)
    lasts = [
        remote(outbox.at[lax.rem(y + d, MESH_Y)], landed.at[y], ls.at[d - 1], lr.at[d - 1], in_group[d - 1])
        for d in range(1, MESH_Y)
    ]
    for copy in lasts:
        copy.start()
    landed[y] = outbox[y]
    weights.wait_recv()
    for copy in lasts:
        copy.wait_recv()

    order = [lax.rem(x + d, MESH_X) for d in (2, 1, 3, 0)]

    def send(src, dst, ssem, rsem, device):
        copy = remote(src, dst, ssem, rsem, device)
        copy.start()
        return copy

    def norm(i):
        rows = pl.ds(pl.multiple_of(order[i] * L, L), L)
        outs = [out_s[4 * order[i] + h] for h in range(4)]
        attended = [o[:, :L] + mm_exact_right(o[:, L:], landed[h]) for h, o in enumerate(outs)]
        scales = [lax.rsqrt(jnp.mean(a * a, axis=1, keepdims=True) + EPS) for a in attended]
        gates = [gate_ref[rows, L * h : L * h + L].astype(F32) for h in range(4)]
        parts = [
            (a * s * gain_ref[...] * (g / (1.0 + jnp.exp(-g)))).astype(BF16)
            for a, s, g in zip(attended, scales, gates)
        ]
        normed[i] = jnp.concatenate(parts, axis=1)
        rows = pl.ds(pl.multiple_of((1 - c) * ROWS, ROWS), ROWS)
        return send(normed.at[i, rows], nbox.at[i], sc.at[i], rc.at[i], twin)

    def mine(i):
        return normed[i, pl.ds(pl.multiple_of(c * ROWS, ROWS), ROWS), :]

    near, far = slice(0, HALF), slice(HALF, WIDE)
    swaps = [norm(i) for i in range(4)]
    ring = []
    swaps[0].wait_recv()
    ring1[0] = (mm(mine(0), w_ref[:, near]) + mm(nbox[0], w2_ref[:, near])).astype(BF16)
    ring.append(send(ring1.at[0], box1.at[0], s1.at[0], r1.at[0], right))
    ring1[1] = (mm(mine(0), w_ref[:, far]) + mm(nbox[0], w2_ref[:, far])).astype(BF16)
    ring.append(send(ring1.at[1], box1.at[1], s1.at[1], r1.at[1], left))
    for swap in swaps[1:]:
        swap.wait_recv()
    my_rows = jnp.concatenate([mine(1), mine(2), mine(3)], axis=0)
    twin_rows = jnp.concatenate([nbox[1], nbox[2], nbox[3]], axis=0)
    own[:, far] = mm(my_rows, w_ref[:, far]) + mm(twin_rows, w2_ref[:, far])
    ring2[0] = own[0:ROWS, far].astype(BF16)
    ring.append(send(ring2.at[0], box2.at[0], s2.at[0], r2.at[0], right))
    own[:, near] = mm(my_rows, w_ref[:, near]) + mm(twin_rows, w2_ref[:, near])
    ring2[1] = own[ROWS : 2 * ROWS, near].astype(BF16)
    ring.append(send(ring2.at[1], box2.at[1], s2.at[1], r2.at[1], left))
    ring[0].wait_recv()
    ring2[2] = (own[0:ROWS, near] + box1[0].astype(F32)).astype(BF16)
    ring.append(send(ring2.at[2], box2.at[2], s2.at[2], r2.at[2], right))
    ring[1].wait_recv()
    ring2[3] = (own[ROWS : 2 * ROWS, far] + box1[1].astype(F32)).astype(BF16)
    ring.append(send(ring2.at[3], box2.at[3], s2.at[3], r2.at[3], left))
    for copy in ring[2:4]:
        copy.wait_recv()
    sum_far = own[2 * ROWS :, far] + box2[0].astype(F32)
    sum_near = own[2 * ROWS :, near] + box2[1].astype(F32)
    ring[4].wait_recv()
    out_near = (sum_near + box2[2].astype(F32)).astype(BF16)
    lo_ref[:, near] = out_near
    new_logit = mm(out_near, router_ref[near])
    ring[5].wait_recv()
    out_far = (sum_far + box2[3].astype(F32)).astype(BF16)
    lo_ref[:, far] = out_far
    new_logit = new_logit + mm(out_far, router_ref[far])
    new_logp = new_logit - jnp.log(jnp.sum(jnp.exp(new_logit), axis=1, keepdims=True))
    div = old_part - jnp.sum(old_prob * new_logp, axis=1, keepdims=True)
    div_ref[...] = jnp.broadcast_to(div, (ROWS, L)).T[0:1, :]

    for copy in firsts + lasts + swaps + ring + [weights]:
        copy.wait_send()
    for d in range(1, QUAD):

        @pl.when(zq + d < QUAD)
        def _():
            up_copy(d).wait_send()

        @pl.when(z == d)
        def _():
            down_copy(d).wait_send()

    for end, served in serves:

        @pl.when(z == end)
        def _():
            for i, other in enumerate(served):
                half_copy(i, other).wait_send()


def layer(*arrays):
    vm = pl.BlockSpec(memory_space=pltpu.VMEM)
    square = (MESH_Y, L, L)
    many = pltpu.VMEM((16, L, L), F32)
    wide = pltpu.VMEM((16, L, 2 * L), F32)
    dma = pltpu.SemaphoreType.DMA
    return pl.pallas_call(
        layer_kernel,
        out_shape=(
            jax.ShapeDtypeStruct((ROWS, WIDE), BF16),
            jax.ShapeDtypeStruct((1, ROWS), F32),
        ),
        in_specs=[pl.BlockSpec(memory_space=pltpu.HBM)] * 11,
        out_specs=(vm, vm),
        scratch_shapes=[
            pltpu.SMEM((4,), jnp.int32),
            pltpu.VMEM((1, L), F32),
            pltpu.VMEM((512, 256), BF16),
            pltpu.VMEM((512, 256), BF16),
            pltpu.VMEM((512, 512), BF16),
            pltpu.VMEM((4, 512), F32),
            pltpu.VMEM((4, 512), F32),
            pltpu.VMEM((512, 512), BF16),
            pltpu.VMEM((512, WIDE), BF16),
            pltpu.VMEM((512, WIDE), BF16),
            pltpu.VMEM((WIDE, 512), BF16),
            pltpu.VMEM((ROWS, 512), jnp.int32),
            pltpu.VMEM((4, 32, L), F32),
            pltpu.VMEM((4, L, L), F32),
            many, many, many, many, wide, wide,
            pltpu.VMEM((MESH_Y, PACK, 2 * L), BF16),
            pltpu.VMEM((MESH_Y, PACK, 2 * L), BF16),
            pltpu.VMEM((MESH_Y - 1, L, 2 * L), F32),
            pltpu.VMEM((PACK, 2 * L), BF16),
            pltpu.VMEM((QUAD, PACK, 2 * L), BF16),
            pltpu.VMEM((L, 2 * L), F32),
            pltpu.VMEM((2, L, L), BF16),
            pltpu.VMEM((L, L), F32),
            pltpu.VMEM(square, BF16),
            pltpu.VMEM(square, BF16),
            pltpu.VMEM((4, L, 512), BF16),
            pltpu.VMEM((4, ROWS, 512), BF16),
            pltpu.VMEM((3 * ROWS, WIDE), F32),
            pltpu.VMEM((2, ROWS, HALF), BF16),
            pltpu.VMEM((2, ROWS, HALF), BF16),
            pltpu.VMEM((4, ROWS, HALF), BF16),
            pltpu.VMEM((4, ROWS, HALF), BF16),
            dma((11,)),
            dma((3,)), dma((3,)),
            dma((QUAD,)), dma((2 * QUAD - 2,)),
            dma((2,)), dma((1,)),
            dma((3,)), dma((3,)),
            dma((1,)), dma((1,)),
            dma((4,)), dma((4,)), dma((2,)), dma((2,)), dma((4,)), dma((4,)),
        ],
        compiler_params=pltpu.CompilerParams(
            collective_id=0, has_side_effects=True, vmem_limit_bytes=36 * 1024 * 1024
        ),
    )(*arrays)


def solution(mesh):
    def local(
        queries, key_vec, values, out_gate, beta_logit, decay_gate, decay_exp,
        norm_gain, out_weight, router_weight, old_scores,
    ):
        arrays = (
            decay_exp, norm_gain.reshape(1, L), queries, key_vec, values, beta_logit, decay_gate,
            out_gate, out_weight, router_weight, old_scores,
        )
        layer_out, div = layer(*(pltpu.with_memory_space_constraint(a, pltpu.HBM) for a in arrays))
        return layer_out, div.reshape(ROWS)

    placed = (
        P("ctx", "head"), P("ctx", "head"), P("ctx", "head"), P("ctx", "head"), P("head", "ctx"),
        P("head", "ctx"), P("head"), P(), P("head", None), P(), P(("ctx", "head"), None),
    )
    return jax.shard_map(
        local,
        mesh=mesh,
        in_specs=placed,
        out_specs=(P(("ctx", "head"), None), P(("ctx", "head"))),
        check_vma=False,
    )
```

time: 55.1 us -> 45.8 us (0.83)
  the two profiles are of different devices: /device:TPU:192 before, /device:TPU:160 now
where the time goes in v3:
time: 45.8 us; the launch traced here: 45.7 us
  Pallas kernels  43.8 us (96%)
  local copies, waits for them, and re-layouts  1.22 us (3%)
  between operations  0.64 us (1%)
    pallas_call x1, Pallas kernels, layer(): pl.pallas_call(layer_kernel, out_shape=(jax.ShapeDtypeStruct((ROWS, WIDE)...  43.8 us
    unnamed x2, local copies, waits for them, and re-layouts  1.22 us

profile of v3, /device:TPU:160, one launch (start us, length us, event | category | flops | bytes accessed | tf_op | source)
XLA Modules:
  0.0 45.7 jit_solution(4767344380961805658)
XLA Ops:
  0.6 43.8 %shard_map.122 = (bf16[64,2048]{1,0:T(8,128)(2,1)S(1)}, f32[1,64]{1,0:T(1,128)S(1)}) custom-call(s32[4]{0:T(128)} %de_hbm.1, f32[1,128]{1,0:T(1,128)} %bitcast.3, bf16[512,256]{1,0:T(8,128)(2,1)} %q_hbm.1, bf16[512,256]{1,0:T(8,128)(2,1)} %k_hbm.1, bf16[512,512]{1,0:T(8,128)(2,1)} %v_hbm.1, f32[4,512]{1,0:T(4,128)} %bl_hbm.1, f32[4,512]{1,0:T(4,128)} %dg_hbm.1, ...), custom_call_target="tpu_custom_call" | custom-call | tf_op jit(solution)/shard_map/pallas_call | solution.py:547
  44.5 0.7 %copy.15 = bf16[64,2048]{1,0:T(8,128)(2,1)} copy(bf16[64,2048]{1,0:T(8,128)(2,1)S(1)} %get-tuple-element.8) | data formatting | bytes 524288
  45.2 0.5 %copy.16 = f32[64]{0:T(128)} copy(f32[64]{0:T(128)S(1)} %bitcast.2) | data formatting | bytes 512

commit v4 on v3

--- a/solution.py
+++ b/solution.py
@@ -93,6 +93,7 @@
 ROWS = 64
 WIDE = 2048
 HALF = WIDE // 2
+QUARTER = WIDE // 4
 MESH_X = 4
 MESH_Y = 4
 QUAD = 4
@@ -145,7 +146,7 @@
         cols_s[b] = jnp.concatenate(parts + [jnp.exp(last - now)] + padding, axis=0).T
 
 
-def solve_blocks(blocks, q_ref, k_ref, v_ref, rows_s, cols_s, t1_s, fade_s, b_s, d_s):
+def solve_blocks(blocks, k_ref, v_ref, rows_s, cols_s, t1_s, fade_s, b_s, d_s, values_ready):
     row, lane = iotas()
     eye = jnp.where(row == lane, 1.0, 0.0).astype(F32)
     tokens = [pl.ds(pl.multiple_of(b * L, L), L) for b in blocks]
@@ -178,6 +179,7 @@
     for (n, h), t1, reach in zip(spots, t1s, reaches):
         t1_s[4 * blocks[n] + h] = t1
         rows_s[blocks[n], 4 + h : 5 + h] = reach
+    values_ready()
     written = [mm_exact_right(t1, v_ref[tokens[n], L * h : L * h + L]) for t1, (n, h) in zip(t1s, spots)]
     widened = [
         mm_exact_right(t1 * reach, keys[2 * n + h // 2]) for t1, reach, (n, h) in zip(t1s, reaches, spots)
@@ -193,11 +195,10 @@
         b_s[4 * blocks[n] + h] = eye * rows[n][24 + h : 25 + h] - change[:, L:]
 
 
-def output_block(b, q_ref, k_ref, v_ref, rows_s, cols_s, t1_s, fade_s, state_s, out_s):
+def output_block(b, q_ref, k_ref, v_ref, rows_s, cols_s, t1_s, fade_s, state_s, out_s, map_s):
     row, lane = iotas()
     tokens = pl.ds(pl.multiple_of(b * L, L), L)
     rows, columns = rows_s[b], cols_s[b]
-    zero = jnp.zeros((L, L), F32)
     keys, queries, scales, grams = [], [], [], []
     for kh in range(2):
         key = k_ref[tokens, L * kh : L * kh + L]
@@ -215,7 +216,9 @@
     from_keys = [mm_exact_right(r * rows[4 + h : 5 + h], keys[h // 2]) for h, r in enumerate(reads)]
     for h in range(4):
         lead = queries[h // 2] * (columns[:, 16 + h : 17 + h] * scales[h // 2]) - from_keys[h]
-        out_s[4 * b + h] = mm_three(lead, state_s[4 * b + h]) + jnp.concatenate([from_values[h], zero], axis=1)
+        both = mm_three(lead, state_s[4 * b + h])
+        out_s[4 * b + h] = both[:, :L] + from_values[h]
+        map_s[4 * b + h] = jnp.concatenate(split(both[:, L:]), axis=1)
 
 
 def pack(state):
@@ -265,10 +268,10 @@
     de_hbm, gain_hbm, q_hbm, k_hbm, v_hbm, bl_hbm, dg_hbm, gate_hbm, w_hbm, router_hbm, old_hbm,
     lo_ref, div_ref,
     de_ref, gain_ref, q_ref, k_ref, v_ref, bl_ref, dg_ref, gate_ref, w_ref, w2_ref, router_ref, old_ref,
-    rows_s, cols_s, t1_s, fade_s, b_s, d_s, state_s, out_s,
-    packs, gath, prefix, total, zbox, acc, first_half, start, outbox, landed,
-    normed, nbox, own, ring1, box1, ring2, box2,
-    load, ys, yr, zs, zr, hs, hr, ls, lr, ws, wr, sc, rc, s1, r1, s2, r2,
+    rows_s, cols_s, t1_s, fade_s, b_s, d_s, state_s, out_s, map_s,
+    packs, gath, prefix, total, zbox, acc, first_half, starts, outbox, landed,
+    gate_s, normed, nbox, ahead, own, ring1, box1, ring2, box2, ring3, box3,
+    load, ys, yr, zs, zr, hs, hr, ls, lr, ws, wr, sc, rc, s1, r1, s2, r2, s3, r3,
 ):
     ctx = lax.axis_index("ctx")
     z, y = ctx // MESH_Y, lax.rem(ctx, MESH_Y)
@@ -293,7 +296,7 @@
             )
         )
     ]
-    for copy in loads:
+    for copy in loads[:6]:
         copy.start()
 
     barrier = pltpu.get_barrier_semaphore()
@@ -318,9 +321,10 @@
     for copy in loads[:3]:
         copy.wait()
     decay_tables(de_ref, bl_ref, dg_ref, rows_s, cols_s)
-    for copy in loads[3:5]:
-        copy.wait()
-    solve_blocks(range(4), q_ref, k_ref, v_ref, rows_s, cols_s, t1_s, fade_s, b_s, d_s)
+    loads[3].wait()
+    for copy in loads[6:]:
+        copy.start()
+    solve_blocks(range(4), k_ref, v_ref, rows_s, cols_s, t1_s, fade_s, b_s, d_s, loads[4].wait)
 
     row, lane = iotas()
     zero = jnp.zeros((L, L), F32)
@@ -357,8 +361,8 @@
         remote(packs.at[lax.rem(y + d, MESH_Y)], gath.at[y], ys.at[d - 1], yr.at[d - 1], in_group[d - 1])
         for d in range(1, MESH_Y)
     ]
-    for copy in firsts:
-        copy.start()
+    for i in (1, 0, 2):
+        firsts[i].start()
     gath[y] = packs[y]
     loads[6].wait()
     weights = remote(w_ref, w2_ref, ws.at[0], wr.at[0], twin)
@@ -366,17 +370,17 @@
     loads[5].wait()
 
     def output(b, carry):
-        output_block(b, q_ref, k_ref, v_ref, rows_s, cols_s, t1_s, fade_s, state_s, out_s)
+        output_block(b, q_ref, k_ref, v_ref, rows_s, cols_s, t1_s, fade_s, state_s, out_s, map_s)
         return carry
 
     lax.fori_loop(0, 4, output, 0)
 
     for copy in firsts:
         copy.wait_recv()
-    state = unpack(gath[0])
-    for j in range(1, MESH_Y):
-        prefix[j - 1] = state
-        state = after(gath[j], state)
+    prefix[0] = unpack(gath[0])
+    prefix[1] = after(gath[1], prefix[0])
+    upper = after(gath[3], unpack(gath[2]))
+    state = mm_three(upper[:, L:], prefix[1]) + jnp.concatenate([upper[:, :L], zero], axis=1)
     total[...] = pack(state)
 
     def up_copy(d):
@@ -386,7 +390,7 @@
     def down_copy(d):
         return remote(total, zbox.at[zq], zs.at[QUAD - 1], zr.at[QUAD - 2 + d], at_z(0))
 
-    for d in range(1, QUAD):
+    for d in range(QUAD - 1, 0, -1):
 
         @pl.when(zq + d < QUAD)
         def _():
@@ -396,30 +400,64 @@
         def _():
             down_copy(d).start()
 
+    prefix[2] = after(gath[2], prefix[1])
     for copy in loads[7:]:
         copy.wait()
+    gain = jnp.concatenate([gain_ref[...]] * 4, axis=1)
+    for b in range(4):
+        gate = gate_ref[L * b : L * b + L, :].astype(F32)
+        gate_s[L * b : L * b + L, :] = gain * (gate / (1.0 + jnp.exp(-gate)))
     old_logit = old_ref[...].astype(F32) / 1024.0
     old_logp = old_logit - jnp.log(jnp.sum(jnp.exp(old_logit), axis=1, keepdims=True))
     old_prob = jnp.exp(old_logp)
     old_part = jnp.sum(old_prob * old_logp, axis=1, keepdims=True)
 
+    def half_copy(i, other):
+        return remote(first_half.at[0], first_half.at[1], hs.at[i], hr.at[0], at_z(other))
+
+    @pl.when(z == QUAD - 1)
+    def _():
+        reach = state
+        for d in range(1, QUAD - 1):
+            up_copy(d).wait_recv()
+            reach = before(reach, zbox[QUAD - 1 - d])
+        up_copy(QUAD - 1).wait_recv()
+        first_half[0] = (reach[:, :L] + mm_exact_right(reach[:, L:], zbox[0, :L, :L])).astype(BF16)
+        for i, other in enumerate(serves[0][1]):
+            half_copy(i, other).start()
+
     acc[...] = jnp.concatenate([zero, eye], axis=1)
     for d in range(1, QUAD):
 
         @pl.when(zq - d >= 0)
         def _():
-            up_copy(d).wait_recv()
+            @pl.when(z != QUAD - 1)
+            def _():
+                up_copy(d).wait_recv()
+
             acc[...] = unpack(zbox[zq - 1]) if d == 1 else before(acc[...], zbox[zq - d])
 
-    def half_copy(i, other):
-        return remote(first_half.at[0], first_half.at[1], hs.at[i], hr.at[0], at_z(other))
-
-    @pl.when(z == QUAD - 1)
+    starts[0:L] = acc[...]
+    moved = mm_three(jnp.concatenate([prefix[j, :, L:] for j in range(MESH_Y - 1)], axis=0), acc[...])
+    for j in range(1, MESH_Y):
+        rows = slice(L * j, L * j + L)
+        starts[rows, :L] = moved[L * (j - 1) : L * j, :L] + prefix[j - 1, :, :L]
+        starts[rows, L:] = moved[L * (j - 1) : L * j, L:]
+
+    @pl.when(z >= QUAD)
     def _():
-        ended = state[:, :L] + mm_three(state[:, L:], acc[:, :L])
-        first_half[0] = ended.astype(BF16)
-        for i, other in enumerate(serves[0][1]):
-            half_copy(i, other).start()
+        half_copy(0, QUAD).wait_recv()
+        starts[:, :L] = starts[:, :L] + mm_exact_right(starts[:, L:], first_half[1])
+
+    for j in range(MESH_Y):
+        outbox[j] = starts[L * j : L * j + L, :L].astype(BF16)
+    lasts = [
+        remote(outbox.at[lax.rem(y + d, MESH_Y)], landed.at[y], ls.at[d - 1], lr.at[d - 1], in_group[d - 1])
+        for d in range(1, MESH_Y)
+    ]
+    for i in (1, 0, 2):
+        lasts[i].start()
+    landed[y] = outbox[y]
 
     @pl.when(z == 0)
     def _():
@@ -431,25 +469,6 @@
         for i, other in enumerate(serves[1][1]):
             half_copy(i, other).start()
 
-    start[...] = acc[:, :L]
-
-    @pl.when(z >= QUAD)
-    def _():
-        half_copy(0, QUAD).wait_recv()
-        start[...] = acc[:, :L] + mm_exact_right(acc[:, L:], first_half[1])
-
-    incoming = start[...]
-    outbox[0] = incoming.astype(BF16)
-    moved = mm_three(jnp.concatenate([prefix[j, :, L:] for j in range(MESH_Y - 1)], axis=0), incoming)
-    for j in range(1, MESH_Y):
-        outbox[j] = (prefix[j - 1, :, :L] + moved[L * (j - 1) : L * j]).astype(BF16)
-    lasts = [
-        remote(outbox.at[lax.rem(y + d, MESH_Y)], landed.at[y], ls.at[d - 1], lr.at[d - 1], in_group[d - 1])
-        for d in range(1, MESH_Y)
-    ]
-    for copy in lasts:
-        copy.start()
-    landed[y] = outbox[y]
     weights.wait_recv()
     for copy in lasts:
         copy.wait_recv()
@@ -463,13 +482,13 @@
 
     def norm(i):
         rows = pl.ds(pl.multiple_of(order[i] * L, L), L)
-        outs = [out_s[4 * order[i] + h] for h in range(4)]
-        attended = [o[:, :L] + mm_exact_right(o[:, L:], landed[h]) for h, o in enumerate(outs)]
+        attended = [
+            out_s[4 * order[i] + h] + mm(map_s[4 * order[i] + h], landed_twice[h]) for h in range(4)
+        ]
         scales = [lax.rsqrt(jnp.mean(a * a, axis=1, keepdims=True) + EPS) for a in attended]
-        gates = [gate_ref[rows, L * h : L * h + L].astype(F32) for h in range(4)]
         parts = [
-            (a * s * gain_ref[...] * (g / (1.0 + jnp.exp(-g)))).astype(BF16)
-            for a, s, g in zip(attended, scales, gates)
+            (a * s * gate_s[rows, L * h : L * h + L]).astype(BF16)
+            for h, (a, s) in enumerate(zip(attended, scales))
         ]
         normed[i] = jnp.concatenate(parts, axis=1)
         rows = pl.ds(pl.multiple_of((1 - c) * ROWS, ROWS), ROWS)
@@ -478,47 +497,49 @@
     def mine(i):
         return normed[i, pl.ds(pl.multiple_of(c * ROWS, ROWS), ROWS), :]
 
+    landed_twice = [jnp.concatenate([landed[h], landed[h]], axis=0) for h in range(4)]
     near, far = slice(0, HALF), slice(HALF, WIDE)
-    swaps = [norm(i) for i in range(4)]
-    ring = []
+    quarters = [slice(QUARTER * n, QUARTER * n + QUARTER) for n in range(4)]
+    swaps = [norm(0)]
+    for cols in quarters:
+        ahead[:, cols] = mm(mine(0), w_ref[:, cols])
+    swaps += [norm(i) for i in range(1, 4)]
     swaps[0].wait_recv()
-    ring1[0] = (mm(mine(0), w_ref[:, near]) + mm(nbox[0], w2_ref[:, near])).astype(BF16)
-    ring.append(send(ring1.at[0], box1.at[0], s1.at[0], r1.at[0], right))
-    ring1[1] = (mm(mine(0), w_ref[:, far]) + mm(nbox[0], w2_ref[:, far])).astype(BF16)
-    ring.append(send(ring1.at[1], box1.at[1], s1.at[1], r1.at[1], left))
+    first = [None] * 4
+    for n in (0, 2, 1, 3):
+        ring1[n] = (ahead[:, quarters[n]] + mm(nbox[0], w2_ref[:, quarters[n]])).astype(BF16)
+        first[n] = send(ring1.at[n], box1.at[n], s1.at[n], r1.at[n], right if n < 2 else left)
     for swap in swaps[1:]:
         swap.wait_recv()
     my_rows = jnp.concatenate([mine(1), mine(2), mine(3)], axis=0)
     twin_rows = jnp.concatenate([nbox[1], nbox[2], nbox[3]], axis=0)
     own[:, far] = mm(my_rows, w_ref[:, far]) + mm(twin_rows, w2_ref[:, far])
     ring2[0] = own[0:ROWS, far].astype(BF16)
-    ring.append(send(ring2.at[0], box2.at[0], s2.at[0], r2.at[0], right))
+    plain = [send(ring2.at[0], box2.at[0], s2.at[0], r2.at[0], right)]
     own[:, near] = mm(my_rows, w_ref[:, near]) + mm(twin_rows, w2_ref[:, near])
     ring2[1] = own[ROWS : 2 * ROWS, near].astype(BF16)
-    ring.append(send(ring2.at[1], box2.at[1], s2.at[1], r2.at[1], left))
-    ring[0].wait_recv()
-    ring2[2] = (own[0:ROWS, near] + box1[0].astype(F32)).astype(BF16)
-    ring.append(send(ring2.at[2], box2.at[2], s2.at[2], r2.at[2], right))
-    ring[1].wait_recv()
-    ring2[3] = (own[ROWS : 2 * ROWS, far] + box1[1].astype(F32)).astype(BF16)
-    ring.append(send(ring2.at[3], box2.at[3], s2.at[3], r2.at[3], left))
-    for copy in ring[2:4]:
+    plain.append(send(ring2.at[1], box2.at[1], s2.at[1], r2.at[1], left))
+    second = [None] * 4
+    for n in (0, 2, 1, 3):
+        first[n].wait_recv()
+        rows = slice(0, ROWS) if n < 2 else slice(ROWS, 2 * ROWS)
+        ring3[n] = (own[rows, quarters[n]] + box1[n].astype(F32)).astype(BF16)
+        second[n] = send(ring3.at[n], box3.at[n], s3.at[n], r3.at[n], right if n < 2 else left)
+    for copy in plain:
         copy.wait_recv()
-    sum_far = own[2 * ROWS :, far] + box2[0].astype(F32)
-    sum_near = own[2 * ROWS :, near] + box2[1].astype(F32)
-    ring[4].wait_recv()
-    out_near = (sum_near + box2[2].astype(F32)).astype(BF16)
-    lo_ref[:, near] = out_near
-    new_logit = mm(out_near, router_ref[near])
-    ring[5].wait_recv()
-    out_far = (sum_far + box2[3].astype(F32)).astype(BF16)
-    lo_ref[:, far] = out_far
-    new_logit = new_logit + mm(out_far, router_ref[far])
+    own[2 * ROWS :, far] = own[2 * ROWS :, far] + box2[0].astype(F32)
+    own[2 * ROWS :, near] = own[2 * ROWS :, near] + box2[1].astype(F32)
+    new_logit = jnp.zeros((ROWS, 512), F32)
+    for n in (0, 2, 1, 3):
+        second[n].wait_recv()
+        done = (own[2 * ROWS :, quarters[n]] + box3[n].astype(F32)).astype(BF16)
+        lo_ref[:, quarters[n]] = done
+        new_logit = new_logit + mm(done, router_ref[quarters[n]])
     new_logp = new_logit - jnp.log(jnp.sum(jnp.exp(new_logit), axis=1, keepdims=True))
     div = old_part - jnp.sum(old_prob * new_logp, axis=1, keepdims=True)
     div_ref[...] = jnp.broadcast_to(div, (ROWS, L)).T[0:1, :]
 
-    for copy in firsts + lasts + swaps + ring + [weights]:
+    for copy in firsts + lasts + swaps + first + plain + second + [weights]:
         copy.wait_send()
     for d in range(1, QUAD):
 
@@ -567,7 +588,8 @@
             pltpu.VMEM((ROWS, 512), jnp.int32),
             pltpu.VMEM((4, 32, L), F32),
             pltpu.VMEM((4, L, L), F32),
-            many, many, many, many, wide, wide,
+            many, many, many, many, wide, many,
+            pltpu.VMEM((16, L, 2 * L), BF16),
             pltpu.VMEM((MESH_Y, PACK, 2 * L), BF16),
             pltpu.VMEM((MESH_Y, PACK, 2 * L), BF16),
             pltpu.VMEM((MESH_Y - 1, L, 2 * L), F32),
@@ -575,23 +597,27 @@
             pltpu.VMEM((QUAD, PACK, 2 * L), BF16),
             pltpu.VMEM((L, 2 * L), F32),
             pltpu.VMEM((2, L, L), BF16),
-            pltpu.VMEM((L, L), F32),
+            pltpu.VMEM((MESH_Y * L, 2 * L), F32),
             pltpu.VMEM(square, BF16),
             pltpu.VMEM(square, BF16),
+            pltpu.VMEM((512, 512), F32),
             pltpu.VMEM((4, L, 512), BF16),
             pltpu.VMEM((4, ROWS, 512), BF16),
+            pltpu.VMEM((ROWS, WIDE), F32),
             pltpu.VMEM((3 * ROWS, WIDE), F32),
+            pltpu.VMEM((4, ROWS, QUARTER), BF16),
+            pltpu.VMEM((4, ROWS, QUARTER), BF16),
             pltpu.VMEM((2, ROWS, HALF), BF16),
             pltpu.VMEM((2, ROWS, HALF), BF16),
-            pltpu.VMEM((4, ROWS, HALF), BF16),
-            pltpu.VMEM((4, ROWS, HALF), BF16),
+            pltpu.VMEM((4, ROWS, QUARTER), BF16),
+            pltpu.VMEM((4, ROWS, QUARTER), BF16),
             dma((11,)),
             dma((3,)), dma((3,)),
             dma((QUAD,)), dma((2 * QUAD - 2,)),
             dma((2,)), dma((1,)),
             dma((3,)), dma((3,)),
             dma((1,)), dma((1,)),
-            dma((4,)), dma((4,)), dma((2,)), dma((2,)), dma((4,)), dma((4,)),
+            dma((4,)), dma((4,)), dma((4,)), dma((4,)), dma((2,)), dma((2,)), dma((4,)), dma((4,)),
         ],
         compiler_params=pltpu.CompilerParams(
             collective_id=0, has_side_effects=True, vmem_limit_bytes=36 * 1024 * 1024

time: 45.8 us -> 42.9 us (0.937)
  the two profiles are of different devices: /device:TPU:160 before, /device:TPU:192 now
where the time goes in v4:
time: 42.9 us; the launch traced here: 42.8 us
  Pallas kernels  41 us (96%)
  local copies, waits for them, and re-layouts  1.22 us (3%)
  between operations  0.64 us (1%)
    pallas_call x1, Pallas kernels, layer(): pl.pallas_call(layer_kernel, out_shape=(jax.ShapeDtypeStruct((ROWS, WIDE)...  41 us
    unnamed x2, local copies, waits for them, and re-layouts  1.22 us

profile of v4, /device:TPU:192, one launch (start us, length us, event | category | flops | bytes accessed | tf_op | source)
XLA Modules:
  0.0 42.8 jit_solution(9160525015116726259)
XLA Ops:
  0.6 41.0 %shard_map.122 = (bf16[64,2048]{1,0:T(8,128)(2,1)S(1)}, f32[1,64]{1,0:T(1,128)S(1)}) custom-call(s32[4]{0:T(128)} %de_hbm.1, f32[1,128]{1,0:T(1,128)} %bitcast.3, bf16[512,256]{1,0:T(8,128)(2,1)} %q_hbm.1, bf16[512,256]{1,0:T(8,128)(2,1)} %k_hbm.1, bf16[512,512]{1,0:T(8,128)(2,1)} %v_hbm.1, f32[4,512]{1,0:T(4,128)} %bl_hbm.1, f32[4,512]{1,0:T(4,128)} %dg_hbm.1, ...), custom_call_target="tpu_custom_call" | custom-call | tf_op jit(solution)/shard_map/pallas_call | solution.py:568
  41.6 0.7 %copy.15 = bf16[64,2048]{1,0:T(8,128)(2,1)} copy(bf16[64,2048]{1,0:T(8,128)(2,1)S(1)} %get-tuple-element.8) | data formatting | bytes 524288
  42.3 0.5 %copy.16 = f32[64]{0:T(128)} copy(f32[64]{0:T(128)S(1)} %bitcast.2) | data formatting | bytes 512

commit v5 on v4

--- a/solution.py
+++ b/solution.py
@@ -29,10 +29,10 @@
     return r[:, :n] + r[:, n:]
 
 
-def mm_rows(a, b):
-    n, wide = a.shape[0], b.shape[1]
-    r = mm(jnp.concatenate(split(a), axis=0), jnp.concatenate(split(b), axis=1))
-    return r[:n, :wide] + (r[:n, wide:] + r[n:, :wide])
+def four_products(a, b):
+    row = jnp.concatenate(b, axis=1)
+    r = mm(jnp.concatenate(a, axis=1), jnp.concatenate([row, row], axis=0))
+    return r[:, :L] + r[:, L:]
 
 
 def mm_three(a, b):
@@ -50,6 +50,17 @@
     if s == 64:
         return x[64:]
     return jnp.concatenate([x[i : i + s] for i in range(s, L, 2 * s)], axis=0)
+
+
+def even_rows(x, s):
+    return jnp.concatenate([x[i : i + s] for i in range(0, L, 2 * s)], axis=0)
+
+
+def interleave(even, odd, s):
+    parts = []
+    for i in range(0, L // 2, s):
+        parts += [even[i : i + s], odd[i : i + s]]
+    return jnp.concatenate(parts, axis=0)
 
 
 def weave(even, odd, s):
@@ -79,14 +90,28 @@
     lane = lax.broadcasted_iota(jnp.int32, (L, L), 1)
     same = row // 16 == lane // 16
     inverses = [jnp.where(same, jnp.concatenate([r] * (L // 16), axis=0), 0.0) for r in solved]
+    halves = [split(t) for t in inverses]
+    twos = range(0, len(systems), 2)
     for s in (16, 32, 64):
         below = odd_rows(row // s, s) == odd_rows(lane // s, s) + 1
-        zeros = jnp.zeros((L, L), F32)
-        lower = [mm_rows(jnp.where(below, odd_rows(a, s), 0.0), t) for a, t in zip(systems, inverses)]
-        full = [weave(zeros, y, s) for y in lower]
-        odd = [odd_rows(t, s) for t in inverses]
-        change = [mm_rows(o, f) for o, f in zip(odd, full)]
-        inverses = [weave(t, o - c, s) for t, o, c in zip(inverses, odd, change)]
+        lower = []
+        for n in twos:
+            one, two = (jnp.where(below, odd_rows(a, s), 0.0) for a in systems[n : n + 2])
+            left = split(jnp.concatenate([one, pltpu.roll(two, s, 1)], axis=0))
+            right = [interleave(even_rows(p, s), even_rows(q, s), s) for p, q in zip(halves[n], halves[n + 1])]
+            lower.append(four_products(left, right))
+        change = []
+        for n, y in zip(twos, lower):
+            one, two = (odd_rows(t, s) for t in inverses[n : n + 2])
+            left = split(jnp.concatenate([one, pltpu.roll(two, L - s, 1)], axis=0))
+            right = [interleave(p[L // 2 :], p[: L // 2], s) for p in split(y)]
+            change.append(four_products(left, right))
+        fresh = []
+        for n, c in zip(twos, change):
+            fresh += [odd_rows(inverses[n], s) - c[: L // 2], odd_rows(inverses[n + 1], s) - c[L // 2 :]]
+        inverses = [weave(t, f, s) for t, f in zip(inverses, fresh)]
+        if s < 64:
+            halves = [[weave(p, q, s) for p, q in zip(half, split(f))] for half, f in zip(halves, fresh)]
     return inverses
 
 
@@ -266,7 +291,7 @@
 
 def layer_kernel(
     de_hbm, gain_hbm, q_hbm, k_hbm, v_hbm, bl_hbm, dg_hbm, gate_hbm, w_hbm, router_hbm, old_hbm,
-    lo_ref, div_ref,
+    lo_ref, logit_ref, prob_ref, part_ref,
     de_ref, gain_ref, q_ref, k_ref, v_ref, bl_ref, dg_ref, gate_ref, w_ref, w2_ref, router_ref, old_ref,
     rows_s, cols_s, t1_s, fade_s, b_s, d_s, state_s, out_s, map_s,
     packs, gath, prefix, total, zbox, acc, first_half, starts, outbox, landed,
@@ -299,6 +324,7 @@
     for copy in loads[:6]:
         copy.start()
 
+    zbox[0] = jnp.zeros((PACK, 2 * L), BF16)
     barrier = pltpu.get_barrier_semaphore()
     for device in in_group + [right, left, twin]:
         signal(barrier, device)
@@ -387,12 +413,20 @@
         device = at_z(quad * QUAD + lax.rem(zq + d, QUAD))
         return remote(total, zbox.at[zq], zs.at[d - 1], zr.at[d - 1], device)
 
+    def first_copy(d):
+        part = (pl.ds(0, L), pl.ds(0, L))
+        return remote(total.at[part], zbox.at[(0, *part)], zs.at[d - 1], zr.at[d - 1], at_z(d))
+
     def down_copy(d):
         return remote(total, zbox.at[zq], zs.at[QUAD - 1], zr.at[QUAD - 2 + d], at_z(0))
 
     for d in range(QUAD - 1, 0, -1):
 
-        @pl.when(zq + d < QUAD)
+        @pl.when(z == 0)
+        def _():
+            first_copy(d).start()
+
+        @pl.when(jnp.logical_and(z > 0, zq + d < QUAD))
         def _():
             up_copy(d).start()
 
@@ -410,7 +444,8 @@
     old_logit = old_ref[...].astype(F32) / 1024.0
     old_logp = old_logit - jnp.log(jnp.sum(jnp.exp(old_logit), axis=1, keepdims=True))
     old_prob = jnp.exp(old_logp)
-    old_part = jnp.sum(old_prob * old_logp, axis=1, keepdims=True)
+    prob_ref[...] = old_prob
+    part_ref[...] = jnp.broadcast_to(jnp.sum(old_prob * old_logp, axis=1, keepdims=True), (ROWS, L))
 
     def half_copy(i, other):
         return remote(first_half.at[0], first_half.at[1], hs.at[i], hr.at[0], at_z(other))
@@ -421,7 +456,7 @@
         for d in range(1, QUAD - 1):
             up_copy(d).wait_recv()
             reach = before(reach, zbox[QUAD - 1 - d])
-        up_copy(QUAD - 1).wait_recv()
+        first_copy(QUAD - 1).wait_recv()
         first_half[0] = (reach[:, :L] + mm_exact_right(reach[:, L:], zbox[0, :L, :L])).astype(BF16)
         for i, other in enumerate(serves[0][1]):
             half_copy(i, other).start()
@@ -431,7 +466,11 @@
 
         @pl.when(zq - d >= 0)
         def _():
-            @pl.when(z != QUAD - 1)
+            @pl.when(jnp.logical_and(z == d, d < QUAD - 1))
+            def _():
+                first_copy(d).wait_recv()
+
+            @pl.when(jnp.logical_and(z != QUAD - 1, z != d))
             def _():
                 up_copy(d).wait_recv()
 
@@ -501,14 +540,12 @@
     near, far = slice(0, HALF), slice(HALF, WIDE)
     quarters = [slice(QUARTER * n, QUARTER * n + QUARTER) for n in range(4)]
     swaps = [norm(0)]
-    for cols in quarters:
-        ahead[:, cols] = mm(mine(0), w_ref[:, cols])
-    swaps += [norm(i) for i in range(1, 4)]
     swaps[0].wait_recv()
     first = [None] * 4
     for n in (0, 2, 1, 3):
-        ring1[n] = (ahead[:, quarters[n]] + mm(nbox[0], w2_ref[:, quarters[n]])).astype(BF16)
+        ring1[n] = (mm(mine(0), w_ref[:, quarters[n]]) + mm(nbox[0], w2_ref[:, quarters[n]])).astype(BF16)
         first[n] = send(ring1.at[n], box1.at[n], s1.at[n], r1.at[n], right if n < 2 else left)
+    swaps += [norm(i) for i in range(1, 4)]
     for swap in swaps[1:]:
         swap.wait_recv()
     my_rows = jnp.concatenate([mine(1), mine(2), mine(3)], axis=0)
@@ -535,15 +572,17 @@
         done = (own[2 * ROWS :, quarters[n]] + box3[n].astype(F32)).astype(BF16)
         lo_ref[:, quarters[n]] = done
         new_logit = new_logit + mm(done, router_ref[quarters[n]])
-    new_logp = new_logit - jnp.log(jnp.sum(jnp.exp(new_logit), axis=1, keepdims=True))
-    div = old_part - jnp.sum(old_prob * new_logp, axis=1, keepdims=True)
-    div_ref[...] = jnp.broadcast_to(div, (ROWS, L)).T[0:1, :]
+    logit_ref[...] = new_logit
 
     for copy in firsts + lasts + swaps + first + plain + second + [weights]:
         copy.wait_send()
     for d in range(1, QUAD):
 
-        @pl.when(zq + d < QUAD)
+        @pl.when(z == 0)
+        def _():
+            first_copy(d).wait_send()
+
+        @pl.when(jnp.logical_and(z > 0, zq + d < QUAD))
         def _():
             up_copy(d).wait_send()
 
@@ -569,10 +608,12 @@
         layer_kernel,
         out_shape=(
             jax.ShapeDtypeStruct((ROWS, WIDE), BF16),
-            jax.ShapeDtypeStruct((1, ROWS), F32),
+            jax.ShapeDtypeStruct((ROWS, 512), F32),
+            jax.ShapeDtypeStruct((ROWS, 512), F32),
+            jax.ShapeDtypeStruct((ROWS, L), F32),
         ),
         in_specs=[pl.BlockSpec(memory_space=pltpu.HBM)] * 11,
-        out_specs=(vm, vm),
+        out_specs=(vm,) * 4,
         scratch_shapes=[
             pltpu.SMEM((4,), jnp.int32),
             pltpu.VMEM((1, L), F32),
@@ -625,6 +666,33 @@
     )(*arrays)
 
 
+def close_kernel(lo_ref, logit_ref, prob_ref, part_ref, lo_hbm, div_hbm, div_ref, out):
+    copies = [pltpu.make_async_copy(lo_ref, lo_hbm, out.at[0]), pltpu.make_async_copy(div_ref, div_hbm, out.at[1])]
+    copies[0].start()
+    new_logit = logit_ref[...]
+    new_logp = new_logit - jnp.log(jnp.sum(jnp.exp(new_logit), axis=1, keepdims=True))
+    div = part_ref[:, 0:1] - jnp.sum(prob_ref[...] * new_logp, axis=1, keepdims=True)
+    div_ref[...] = jnp.broadcast_to(div, (ROWS, L)).T[0:1, :]
+    copies[1].start()
+    for copy in copies:
+        copy.wait()
+
+
+def close(*arrays):
+    vm, hbm = pl.BlockSpec(memory_space=pltpu.VMEM), pl.BlockSpec(memory_space=pltpu.HBM)
+    return pl.pallas_call(
+        close_kernel,
+        out_shape=(
+            jax.ShapeDtypeStruct((ROWS, WIDE), BF16),
+            jax.ShapeDtypeStruct((1, ROWS), F32),
+        ),
+        in_specs=[vm] * 4,
+        out_specs=(hbm, hbm),
+        scratch_shapes=[pltpu.VMEM((1, ROWS), F32), pltpu.SemaphoreType.DMA((2,))],
+        compiler_params=pltpu.CompilerParams(vmem_limit_bytes=36 * 1024 * 1024),
+    )(*arrays)
+
+
 def solution(mesh):
     def local(
         queries, key_vec, values, out_gate, beta_logit, decay_gate, decay_exp,
@@ -634,7 +702,7 @@
             decay_exp, norm_gain.reshape(1, L), queries, key_vec, values, beta_logit, decay_gate,
             out_gate, out_weight, router_weight, old_scores,
         )
-        layer_out, div = layer(*(pltpu.with_memory_space_constraint(a, pltpu.HBM) for a in arrays))
+        layer_out, div = close(*layer(*(pltpu.with_memory_space_constraint(a, pltpu.HBM) for a in arrays)))
         return layer_out, div.reshape(ROWS)
 
     placed = (

time: 42.9 us -> 41.3 us (0.963)
  local copies, waits for them, and re-layouts: 1.22 us -> 0 us
  Pallas kernels: 41 us -> 40.5 us
    pallas_call x1, Pallas kernels: 41 us -> 39.7 us  [layer(): pl.pallas_call(layer_kernel, out_shape=(jax.ShapeDtypeStruct((ROWS, WIDE)...]
    unnamed x2 -> x0, local copies, waits for them, and re-layouts: 1.22 us -> none
    pallas_call x0 -> x1, Pallas kernels: none -> 0.86 us  [close(): pl.pallas_call(close_kernel, out_shape=(jax.ShapeDtypeStruct((ROWS, WIDE)...]
where the time goes in v5:
time: 41.3 us; the launch traced here: 41.2 us
  Pallas kernels  40.5 us (98%)
  between operations  0.64 us (2%)
    pallas_call x1, Pallas kernels, layer(): pl.pallas_call(layer_kernel, out_shape=(jax.ShapeDtypeStruct((ROWS, WIDE)...  39.7 us
    pallas_call x1, Pallas kernels, close(): pl.pallas_call(close_kernel, out_shape=(jax.ShapeDtypeStruct((ROWS, WIDE)...  0.86 us

profile of v5, /device:TPU:192, one launch (start us, length us, event | category | flops | bytes accessed | tf_op | source)
XLA Modules:
  0.0 41.2 jit_solution(8260425269994799403)
XLA Ops:
  0.6 39.7 %shard_map.122 = (bf16[64,2048]{1,0:T(8,128)(2,1)S(1)}, f32[64,512]{1,0:T(8,128)S(1)}, f32[64,512]{1,0:T(8,128)S(1)}, f32[64,128]{1,0:T(8,128)S(1)}) custom-call(s32[4]{0:T(128)} %de_hbm.1, f32[1,128]{1,0:T(1,128)} %bitcast.2, bf16[512,256]{1,0:T(8,128)(2,1)} %q_hbm.1, bf16[512,256]{1,0:T(8,128)(2,1)} %k_hbm.1, bf16[512,512]{1,0:T(8,128)(2,1)} %v_hbm.1, ...), custom_call_target="tpu_custom_call" | custom-call | tf_op jit(solution)/shard_map/pallas_call | solution.py:607
  40.3 0.9 %shard_map.123 = (bf16[64,2048]{1,0:T(8,128)(2,1)}, f32[1,64]{1,0:T(1,128)}) custom-call(bf16[64,2048]{1,0:T(8,128)(2,1)S(1)} %get-tuple-element.8.lo_ref, f32[64,512]{1,0:T(8,128)S(1)} %get-tuple-element.9.logit_ref, f32[64,512]{1,0:T(8,128)S(1)} %get-tuple-element.10.prob_ref, f32[64,128]{1,0:T(8,128)S(1)} %get-tuple-element.11.part_ref), custom_call_target="tpu_custom_call" | custom-call | tf_op jit(solution)/shard_map/pallas_call | solution.py:683

commit v6 on v5

--- a/solution.py
+++ b/solution.py
@@ -71,46 +71,51 @@
 
 
 def unit_lower_inverse(systems):
-    lane16 = lax.broadcasted_iota(jnp.int32, (16, L), 1)
-    row16 = lax.broadcasted_iota(jnp.int32, (16, L), 0)
-    place = lane16 // 16
+    lane8 = lax.broadcasted_iota(jnp.int32, (8, L), 1)
+    row8 = lax.broadcasted_iota(jnp.int32, (8, L), 0)
+    place = lane8 // 8
     bands = []
     for a in systems:
-        band = jnp.zeros((16, L), F32)
-        for b in range(L // 16):
-            band = jnp.where(place == b, a[16 * b : 16 * b + 16], band)
+        band = jnp.zeros((8, L), F32)
+        for b in range(L // 8):
+            band = jnp.where(place == b, a[8 * b : 8 * b + 8], band)
         bands.append(band)
-    start = jnp.where(lane16 % 16 == row16, 1.0, 0.0).astype(F32)
+    start = jnp.where(lane8 % 8 == row8, 1.0, 0.0).astype(F32)
     solved = [start for _ in systems]
-    for m in range(15):
-        index = place * 16 + m
+    for m in range(7):
+        index = place * 8 + m
         spread = [jnp.take_along_axis(band, index, axis=1) for band in bands]
         solved = [r - s * r[m : m + 1] for r, s in zip(solved, spread)]
     row = lax.broadcasted_iota(jnp.int32, (L, L), 0)
     lane = lax.broadcasted_iota(jnp.int32, (L, L), 1)
-    same = row // 16 == lane // 16
-    inverses = [jnp.where(same, jnp.concatenate([r] * (L // 16), axis=0), 0.0) for r in solved]
-    halves = [split(t) for t in inverses]
+    same = row // 8 == lane // 8
+    inverses = [jnp.where(same, jnp.concatenate([r] * (L // 8), axis=0), 0.0) for r in solved]
+    halves = [[t] for t in inverses]
     twos = range(0, len(systems), 2)
-    for s in (16, 32, 64):
+    for s in (8, 16, 32, 64):
         below = odd_rows(row // s, s) == odd_rows(lane // s, s) + 1
         lower = []
         for n in twos:
             one, two = (jnp.where(below, odd_rows(a, s), 0.0) for a in systems[n : n + 2])
             left = split(jnp.concatenate([one, pltpu.roll(two, s, 1)], axis=0))
             right = [interleave(even_rows(p, s), even_rows(q, s), s) for p, q in zip(halves[n], halves[n + 1])]
-            lower.append(four_products(left, right))
+            lower.append(four_products(left, right if s > 8 else split(right[0])))
         change = []
         for n, y in zip(twos, lower):
             one, two = (odd_rows(t, s) for t in inverses[n : n + 2])
             left = split(jnp.concatenate([one, pltpu.roll(two, L - s, 1)], axis=0))
-            right = [interleave(p[L // 2 :], p[: L // 2], s) for p in split(y)]
+            if s > 8:
+                right = [interleave(p[L // 2 :], p[: L // 2], s) for p in split(y)]
+            else:
+                right = split(interleave(y[L // 2 :], y[: L // 2], s))
             change.append(four_products(left, right))
         fresh = []
         for n, c in zip(twos, change):
             fresh += [odd_rows(inverses[n], s) - c[: L // 2], odd_rows(inverses[n + 1], s) - c[L // 2 :]]
         inverses = [weave(t, f, s) for t, f in zip(inverses, fresh)]
-        if s < 64:
+        if s == 8:
+            halves = [split(t) for t in inverses]
+        elif s < 64:
             halves = [[weave(p, q, s) for p, q in zip(half, split(f))] for half, f in zip(halves, fresh)]
     return inverses
 
@@ -294,7 +299,7 @@
     lo_ref, logit_ref, prob_ref, part_ref,
     de_ref, gain_ref, q_ref, k_ref, v_ref, bl_ref, dg_ref, gate_ref, w_ref, w2_ref, router_ref, old_ref,
     rows_s, cols_s, t1_s, fade_s, b_s, d_s, state_s, out_s, map_s,
-    packs, gath, prefix, total, zbox, acc, first_half, starts, outbox, landed,
+    packs, gath, prefix, total, zbox, acc, first_half, starts, maps_s, outbox, landed,
     gate_s, normed, nbox, ahead, own, ring1, box1, ring2, box2, ring3, box3,
     load, ys, yr, zs, zr, hs, hr, ls, lr, ws, wr, sc, rc, s1, r1, s2, r2, s3, r3,
 ):
@@ -355,17 +360,17 @@
     row, lane = iotas()
     zero = jnp.zeros((L, L), F32)
     eye = jnp.where(row == lane, 1.0, 0.0).astype(F32)
-    states = []
-    for h in range(4):
-        state_s[h] = jnp.concatenate([zero, eye], axis=1)
-        states.append(jnp.concatenate([d_s[h], b_s[h]], axis=1))
-    for b in range(1, 4):
-        for h in range(4):
-            state_s[4 * b + h] = states[h]
-        states = [
-            mm_three(b_s[4 * b + h], states[h]) + jnp.concatenate([d_s[4 * b + h], zero], axis=1)
-            for h in range(4)
-        ]
+
+    def step(b, h, state):
+        return mm_three(b_s[4 * b + h], state) + jnp.concatenate([d_s[4 * b + h], zero], axis=1)
+
+    early = [jnp.concatenate([d_s[h], b_s[h]], axis=1) for h in range(4)]
+    late = [jnp.concatenate([d_s[8 + h], b_s[8 + h]], axis=1) for h in range(4)]
+    middle = [step(1, h, early[h]) for h in range(4)]
+    late = [step(3, h, late[h]) for h in range(4)]
+    states = [
+        mm_three(q[:, L:], p) + jnp.concatenate([q[:, :L], zero], axis=1) for p, q in zip(middle, late)
+    ]
     for h, packed in enumerate([pack(state) for state in states]):
         packs[h] = packed
 
@@ -394,6 +399,12 @@
     weights = remote(w_ref, w2_ref, ws.at[0], wr.at[0], twin)
     weights.start()
     loads[5].wait()
+
+    for h in range(4):
+        state_s[h] = jnp.concatenate([zero, eye], axis=1)
+        state_s[4 + h] = early[h]
+        state_s[8 + h] = middle[h]
+        state_s[12 + h] = step(2, h, middle[h])
 
     def output(b, carry):
         output_block(b, q_ref, k_ref, v_ref, rows_s, cols_s, t1_s, fade_s, state_s, out_s, map_s)
@@ -483,13 +494,19 @@
         starts[rows, :L] = moved[L * (j - 1) : L * j, :L] + prefix[j - 1, :, :L]
         starts[rows, L:] = moved[L * (j - 1) : L * j, L:]
 
+    @pl.when(z < QUAD)
+    def _():
+        for j in range(MESH_Y):
+            outbox[j] = starts[L * j : L * j + L, :L].astype(BF16)
+
     @pl.when(z >= QUAD)
     def _():
+        maps_s[...] = jnp.concatenate(split(starts[:, L:]), axis=1)
         half_copy(0, QUAD).wait_recv()
-        starts[:, :L] = starts[:, :L] + mm_exact_right(starts[:, L:], first_half[1])
-
-    for j in range(MESH_Y):
-        outbox[j] = starts[L * j : L * j + L, :L].astype(BF16)
+        ended = jnp.concatenate([first_half[1], first_half[1]], axis=0)
+        for j in range(MESH_Y):
+            rows = slice(L * j, L * j + L)
+            outbox[j] = (starts[rows, :L] + mm(maps_s[rows], ended)).astype(BF16)
     lasts = [
         remote(outbox.at[lax.rem(y + d, MESH_Y)], landed.at[y], ls.at[d - 1], lr.at[d - 1], in_group[d - 1])
         for d in range(1, MESH_Y)
@@ -639,6 +656,7 @@
             pltpu.VMEM((L, 2 * L), F32),
             pltpu.VMEM((2, L, L), BF16),
             pltpu.VMEM((MESH_Y * L, 2 * L), F32),
+            pltpu.VMEM((MESH_Y * L, 2 * L), BF16),
             pltpu.VMEM(square, BF16),
             pltpu.VMEM(square, BF16),
             pltpu.VMEM((512, 512), F32),

time: 41.3 us -> 40.9 us (level)
  no operation moved by 1% of the time
where the time goes in v6:
time: 40.9 us; the launch traced here: 40.8 us
  Pallas kernels  40.2 us (98%)
  between operations  0.64 us (2%)
    pallas_call x1, Pallas kernels, layer(): pl.pallas_call(layer_kernel, out_shape=(jax.ShapeDtypeStruct((ROWS, WIDE)...  39.3 us
    pallas_call x1, Pallas kernels, close(): pl.pallas_call(close_kernel, out_shape=(jax.ShapeDtypeStruct((ROWS, WIDE)...  0.86 us

profile of v6, /device:TPU:192, one launch (start us, length us, event | category | flops | bytes accessed | tf_op | source)
XLA Modules:
  0.0 40.8 jit_solution(15053644156369625078)
XLA Ops:
  0.6 39.3 %shard_map.122 = (bf16[64,2048]{1,0:T(8,128)(2,1)S(1)}, f32[64,512]{1,0:T(8,128)S(1)}, f32[64,512]{1,0:T(8,128)S(1)}, f32[64,128]{1,0:T(8,128)S(1)}) custom-call(s32[4]{0:T(128)} %de_hbm.1, f32[1,128]{1,0:T(1,128)} %bitcast.2, bf16[512,256]{1,0:T(8,128)(2,1)} %q_hbm.1, bf16[512,256]{1,0:T(8,128)(2,1)} %k_hbm.1, bf16[512,512]{1,0:T(8,128)(2,1)} %v_hbm.1, ...), custom_call_target="tpu_custom_call" | custom-call | tf_op jit(solution)/shard_map/pallas_call | solution.py:624
  40.0 0.9 %shard_map.123 = (bf16[64,2048]{1,0:T(8,128)(2,1)}, f32[1,64]{1,0:T(1,128)}) custom-call(bf16[64,2048]{1,0:T(8,128)(2,1)S(1)} %get-tuple-element.8.lo_ref, f32[64,512]{1,0:T(8,128)S(1)} %get-tuple-element.9.logit_ref, f32[64,512]{1,0:T(8,128)S(1)} %get-tuple-element.10.prob_ref, f32[64,128]{1,0:T(8,128)S(1)} %get-tuple-element.11.part_ref), custom_call_target="tpu_custom_call" | custom-call | tf_op jit(solution)/shard_map/pallas_call | solution.py:701

commit v7 on v6

--- a/solution.py
+++ b/solution.py
@@ -431,7 +431,7 @@
     def down_copy(d):
         return remote(total, zbox.at[zq], zs.at[QUAD - 1], zr.at[QUAD - 2 + d], at_z(0))
 
-    for d in range(QUAD - 1, 0, -1):
+    for d in range(1, QUAD):
 
         @pl.when(z == 0)
         def _():

time: 40.9 us -> 41.5 us (1.015); the launches traced: 40.8 us -> 40.7 us
  no operation moved by 1% of the time
where the time goes in v7:
time: 41.5 us; the launch traced here: 40.7 us
  Pallas kernels  40.1 us (97%)
  between operations  0.64 us (2%)
    pallas_call x1, Pallas kernels, layer(): pl.pallas_call(layer_kernel, out_shape=(jax.ShapeDtypeStruct((ROWS, WIDE)...  39.2 us
    pallas_call x1, Pallas kernels, close(): pl.pallas_call(close_kernel, out_shape=(jax.ShapeDtypeStruct((ROWS, WIDE)...  0.86 us

profile of v7, /device:TPU:192, one launch (start us, length us, event | category | flops | bytes accessed | tf_op | source)
XLA Modules:
  0.0 40.7 jit_solution(7794125724426513445)
XLA Ops:
  0.6 39.2 %shard_map.122 = (bf16[64,2048]{1,0:T(8,128)(2,1)S(1)}, f32[64,512]{1,0:T(8,128)S(1)}, f32[64,512]{1,0:T(8,128)S(1)}, f32[64,128]{1,0:T(8,128)S(1)}) custom-call(s32[4]{0:T(128)} %de_hbm.1, f32[1,128]{1,0:T(1,128)} %bitcast.2, bf16[512,256]{1,0:T(8,128)(2,1)} %q_hbm.1, bf16[512,256]{1,0:T(8,128)(2,1)} %k_hbm.1, bf16[512,512]{1,0:T(8,128)(2,1)} %v_hbm.1, ...), custom_call_target="tpu_custom_call" | custom-call | tf_op jit(solution)/shard_map/pallas_call | solution.py:624
  39.9 0.9 %shard_map.123 = (bf16[64,2048]{1,0:T(8,128)(2,1)}, f32[1,64]{1,0:T(1,128)}) custom-call(bf16[64,2048]{1,0:T(8,128)(2,1)S(1)} %get-tuple-element.8.lo_ref, f32[64,512]{1,0:T(8,128)S(1)} %get-tuple-element.9.logit_ref, f32[64,512]{1,0:T(8,128)S(1)} %get-tuple-element.10.prob_ref, f32[64,128]{1,0:T(8,128)S(1)} %get-tuple-element.11.part_ref), custom_call_target="tpu_custom_call" | custom-call | tf_op jit(solution)/shard_map/pallas_call | solution.py:701
